TPU v7x, 256 devices: a whole 4x4x8 slice. The times are simulated.
256 devices in a mesh: dp: 8 (over x, core), clus: 32 (over z, y).
Axes of the slice: x: 4, y: 4, z: 8, core: 2. Of those that a mesh axis runs over, the one named last changes fastest.
Arguments:
- activations: bfloat16 [1024, 12288], P('clus', 'dp'), may hold values from -6 to 6
- picks: int32 [1024, 48], replicated, may hold values from 0 to 383, all different within a row
- up_weight: bfloat16 [384, 12288, 128], P('clus', 'dp'), may hold values from -0.0546875 to 0.0546875
- up_bias: float32 [384, 128], P('clus'), may hold values from -3 to 3
- down_weight: bfloat16 [384, 128, 12288], P('clus', None, 'dp'), may hold values from -0.078125 to 0.078125
Outputs:
- layer_out: bfloat16 [1024, 12288], P('clus', 'dp')
Inputs may be any that keep to these rules, and one draw needn't show every extreme that they name: `picks`: each row names 48 distinct clusters; every cluster is named by some row.
All inputs are finite; a program needn't handle non-finite values.
Results may differ from a plain program's by a relative error of at most 0.012.
Values may be sent and summed in bfloat16 or wider, within the bound.
No kernel may reach another device: no remote copies, remote signals or barrier semaphores. Data moves between devices by JAX's collectives and lax.ppermute only.
A program may use at most 64 MiB of HBM per device.

v0:
```python
import jax
import jax.numpy as jnp
from jax import lax
from jax.experimental import pallas as pl
from jax.experimental.pallas import tpu as pltpu
from jax.sharding import Mesh
from jax.sharding import PartitionSpec as P

F32, BF16, I32 = jnp.float32, jnp.bfloat16, jnp.int32
NX, NC, NZ, NY = 4, 2, 8, 4
BLOCKS = NX * NC
SLOTS = 192
PACK = 4
TILE = 512
VMEM = 32 << 20


def spread(block, axis):
    peers = lax.axis_size(axis)
    return lax.all_to_all(
        jnp.broadcast_to(block[None], (peers,) + block.shape), axis, split_axis=0, concat_axis=0
    )


def exchange(blocks, axis):
    return lax.all_to_all(blocks, axis, split_axis=0, concat_axis=0)


def total(blocks):
    return jnp.sum(blocks.astype(F32), axis=0)


def from_peer(block, axis, step):
    n = lax.axis_size(axis)
    return lax.ppermute(block, axis, [((i + step) % n, i) for i in range(n)])


def ring_spread(block, axis, beside):
    n = lax.axis_size(axis)
    found = {0: block}
    for k in range(1, n // 2):
        found[k] = from_peer(found[k - 1], axis, 1)
        found[n - k] = from_peer(found[(n + 1 - k) % n], axis, -1)
    half = block.shape[0] // 2
    low, high = found[n // 2 - 1], found[n // 2 + 1]
    low, high, beside = lax.optimization_barrier((low, high, beside))
    low, high = from_peer(low[:half], axis, 1), from_peer(high[half:], axis, -1)
    found[n // 2] = jnp.concatenate([low, high])
    return jnp.stack([found[k] for k in range(n)]), beside


def ring_total(blocks, axis, beside):
    n, half = blocks.shape[0], blocks.shape[1] // 2
    low = from_peer(blocks[n // 2][:half], axis, 1).astype(F32)
    high = from_peer(blocks[n // 2][half:], axis, -1).astype(F32)
    down, up = blocks[n // 2 + 1], blocks[n // 2 - 1]
    down = jnp.concatenate([(down[:half] + low).astype(BF16), down[half:]])
    up = jnp.concatenate([up[:half], (up[half:] + high).astype(BF16)])
    for k in range(n // 2 - 2, -1, -1):
        if k == 0:
            down, up, beside = lax.optimization_barrier((down, up, beside))
        down, up = from_peer(down, axis, 1).astype(F32), from_peer(up, axis, -1).astype(F32)
        if k > 0:
            down, up = (blocks[n - k] + down).astype(BF16), (blocks[k] + up).astype(BF16)
    return blocks[0] + down + up, beside


def up_kernel(at_ref, x_ref, w_ref, bias_ref, pos_ref, out_ref, acc):
    span, neurons = x_ref.shape[0] // BLOCKS, w_ref.shape[-1]
    slot = lax.broadcasted_iota(I32, (SLOTS, PACK * span), 0)

    @pl.when(pl.program_id(0) == 0)
    def _():
        acc[...] = jnp.zeros_like(acc)

    pairs = []
    for p in range(0, PACK, 2):
        wide = jnp.concatenate([w_ref[p], w_ref[p + 1]], axis=1)
        bias = jnp.concatenate([bias_ref[0, p : p + 1], bias_ref[0, p + 1 : p + 2]], axis=1)
        pre = jnp.dot(x_ref[...], wide, preferred_element_type=F32)
        pairs.append((pre + bias).astype(BF16))
    for b in range(BLOCKS):
        rows = slice(b * span, (b + 1) * span)
        both = jnp.concatenate(
            [p[rows, k * neurons : (k + 1) * neurons] for p in pairs for k in range(2)], axis=0
        )
        take = jnp.where(slot == pos_ref[0, b : b + 1, :], 1.0, 0.0).astype(BF16)
        acc[b] += jnp.dot(take, both, preferred_element_type=F32)

    @pl.when(pl.program_id(0) == pl.num_programs(0) - 1)
    def _():
        for j in range(BLOCKS):
            out_ref[j] = acc[at_ref[j]].astype(BF16)


def packed_up(at, x, up_weight, bias, pos, part):
    clusters, width, neurons = up_weight.shape
    tokens = x.shape[0]
    return pl.pallas_call(
        up_kernel,
        grid_spec=pltpu.PrefetchScalarGridSpec(
            num_scalar_prefetch=1,
            grid=(clusters // PACK,),
            in_specs=[
                pl.BlockSpec((tokens, width), lambda i, at: (0, 0)),
                pl.BlockSpec((PACK, width, neurons), lambda i, at: (i, 0, 0)),
                pl.BlockSpec((1, PACK, neurons), lambda i, at: (i, 0, 0)),
                pl.BlockSpec((1, BLOCKS, PACK * tokens // BLOCKS), lambda i, at: (i, part, 0)),
            ],
            out_specs=pl.BlockSpec((BLOCKS, SLOTS, neurons), lambda i, at: (0, 0, 0)),
            scratch_shapes=[pltpu.VMEM((BLOCKS, SLOTS, neurons), F32)],
        ),
        out_shape=jax.ShapeDtypeStruct((BLOCKS, SLOTS, neurons), BF16),
        compiler_params=pltpu.CompilerParams(vmem_limit_bytes=VMEM),
        cost_estimate=pl.CostEstimate(
            flops=4 * tokens * width * clusters * neurons, bytes_accessed=9 << 20, transcendentals=0
        ),
    )(at, x, up_weight, bias, pos)


def down_kernel(at_ref, packed_ref, pos_ref, w_ref, out_ref, hidden):
    neurons = packed_ref.shape[-1]
    span = hidden.shape[0] // BLOCKS

    @pl.when(pl.program_id(0) == 0)
    def _():
        slot = lax.broadcasted_iota(I32, (SLOTS, PACK * span), 0)
        @pl.loop(0, BLOCKS)
        def _(j):
            b = at_ref[j]
            to = pl.ds(pl.multiple_of(b * span, span), span)
            for q in range(pos_ref.shape[0]):
                take = jnp.where(slot == pos_ref[q, pl.ds(b, 1), :], 1.0, 0.0).astype(BF16)
                both = lax.dot_general(
                    take, packed_ref[j], (((0,), (0,)), ((), ())), preferred_element_type=F32
                ).astype(BF16)
                for k in range(PACK):
                    c = q * PACK + k
                    hidden[to, c * neurons : (c + 1) * neurons] = both[k * span : (k + 1) * span]

    wide = w_ref[...].reshape(-1, w_ref.shape[-1])
    out_ref[...] = jnp.dot(hidden[...], wide, preferred_element_type=F32).astype(BF16)


def packed_down(at, packed, pos, down_weight, tokens, part):
    clusters, neurons, width = down_weight.shape
    return pl.pallas_call(
        down_kernel,
        grid_spec=pltpu.PrefetchScalarGridSpec(
            num_scalar_prefetch=1,
            grid=(width // TILE,),
            in_specs=[
                pl.BlockSpec((BLOCKS, SLOTS, neurons), lambda n, at: (0, part, 0)),
                pl.BlockSpec((pos.shape[0], BLOCKS, pos.shape[2]), lambda n, at: (0, part, 0)),
                pl.BlockSpec((clusters, neurons, TILE), lambda n, at: (0, 0, n)),
            ],
            out_specs=pl.BlockSpec((tokens, TILE), lambda n, at: (0, n)),
            scratch_shapes=[pltpu.VMEM((tokens, clusters * neurons), BF16)],
        ),
        out_shape=jax.ShapeDtypeStruct((tokens, width), BF16),
        compiler_params=pltpu.CompilerParams(vmem_limit_bytes=VMEM),
        cost_estimate=pl.CostEstimate(
            flops=2 * tokens * clusters * neurons * width, bytes_accessed=7 << 20, transcendentals=0
        ),
    )(at, packed, pos, down_weight)


def slots_of(mask):
    clusters, _, span = mask.shape
    hits = mask.astype(BF16)
    before = jnp.triu(jnp.ones((span, span), BF16), 1)
    ahead = jnp.triu(jnp.ones((clusters, clusters), BF16), 1)
    each = jnp.sum(hits.astype(F32), axis=0).astype(BF16)
    base = jnp.dot(each, before, preferred_element_type=F32)
    within = jnp.einsum("kbt,kc->cbt", hits, ahead, preferred_element_type=F32)
    return jnp.where(mask, base[None] + within, -1.0).astype(I32)


def loop_spread(block, axes):
    n, me = lax.axis_size(axes), lax.axis_index(axes)

    def step(k, held):
        block, found = held
        block = from_peer(block, axes, 1)
        return block, lax.dynamic_update_index_in_dim(found, block, (me + k) % n, 0)

    found = lax.dynamic_update_index_in_dim(jnp.zeros((n,) + block.shape, block.dtype), block, me, 0)
    return lax.fori_loop(1, n, step, (block, found))[1]


def loop_total(blocks, axes):
    n, me = lax.axis_size(axes), lax.axis_index(axes)

    def step(k, sum):
        sum = from_peer(sum, axes, 1)
        return sum + lax.dynamic_index_in_dim(blocks, (me + k) % n, 0, False).astype(F32)

    first = lax.dynamic_index_in_dim(blocks, (me + 1) % n, 0, False).astype(F32)
    return lax.fori_loop(2, n + 1, step, first)


def dense(activations, picks, up_weight, up_bias, down_weight):
    rows, width = activations.shape
    clusters, _, neurons = up_weight.shape
    tokens, span = picks.shape[0], picks.shape[0] // BLOCKS
    dp, clus = ("x", "core"), ("z", "y")
    x = loop_spread(activations, clus).reshape(tokens, width)
    picked = lax.dynamic_slice_in_dim(picks, lax.axis_index(dp) * span, span, 0)

    def cluster(c, out):
        part = jnp.dot(x, up_weight[c], preferred_element_type=F32)
        summed = loop_total(part.reshape(BLOCKS, span, neurons), dp) + up_bias[c]
        keep = jnp.any(picked == lax.axis_index(clus) * clusters + c, axis=1, keepdims=True)
        hidden = jnp.where(keep, jnp.maximum(summed, 0.0), 0.0).astype(BF16)
        hidden = loop_spread(hidden, dp).reshape(tokens, neurons)
        return out + jnp.dot(hidden, down_weight[c], preferred_element_type=F32)

    out = lax.fori_loop(0, clusters, cluster, jnp.zeros((tokens, width), F32)).astype(BF16)
    return loop_total(out.reshape(-1, rows, width), clus).astype(BF16)


def on_device(activations, picks, up_weight, up_bias, down_weight):
    rows, width = activations.shape
    clusters, _, neurons = up_weight.shape
    cut = rows // 2
    tokens = NZ * NY * cut
    span = tokens // BLOCKS
    core, xi = lax.axis_index("core"), lax.axis_index("x")
    zi, yi = lax.axis_index("z"), lax.axis_index("y")

    first, second = activations[:cut], activations[cut:]
    first = spread(first, "z")

    wanted = (zi * NY + yi) * clusters + jnp.arange(clusters, dtype=I32)
    mask = jnp.any(picks.T[None, :, :] == wanted[:, None, None], axis=1)
    mask = mask.reshape(clusters, NZ, NY, 2, cut)
    mask_1 = mask[:, :, :, 0].transpose(0, 2, 1, 3).reshape(clusters, BLOCKS, span)
    mask_2 = jnp.roll(mask[:, :, :, 1], (-zi, -yi), axis=(1, 2)).reshape(clusters, BLOCKS, span)
    pos = slots_of(jnp.concatenate([mask_1, mask_2], axis=1))
    pos = pos.reshape(clusters // PACK, PACK, 2 * BLOCKS, span).transpose(0, 2, 1, 3)
    pos = pos.reshape(clusters // PACK, 2 * BLOCKS, PACK * span)

    groups = picks.T // clusters
    named = jnp.sum(
        (groups[None] == jnp.arange(NZ * NY, dtype=I32)[:, None, None]).astype(F32), axis=1
    ).astype(BF16)
    token = jnp.arange(2 * tokens, dtype=I32)
    z, y, part = token // (2 * cut * NY), token // (2 * cut) % NY, token // cut % 2
    block = jnp.where(part == 0, (y * NZ + z) * BLOCKS // (NY * NZ), BLOCKS + z * BLOCKS // NZ)
    belongs = (block[:, None] == jnp.arange(2 * BLOCKS, dtype=I32)[None]).astype(BF16)
    room = jnp.max(jnp.dot(named, belongs, preferred_element_type=F32))

    near = jnp.stack([second] + [from_peer(second, "y", k) for k in range(1, NY)])
    near, first = lax.optimization_barrier((near, first))
    x_1 = spread(first, "y").reshape(tokens, width)
    x_2, (x_1, room) = ring_spread(near, "z", (x_1, room))
    x_2 = x_2.reshape(tokens, width)

    order = [((core + j // NX) % NC) * NX + (xi + j % NX) % NX for j in range(BLOCKS)]
    at = jnp.stack(order).astype(I32)
    bias = (up_bias * (1.0 / BLOCKS)).reshape(clusters // PACK, PACK, neurons)

    def pair_of(x, part):
        rows = packed_up(at, x, up_weight, bias, pos, part)
        return rows[:NX].astype(F32) + from_peer(rows[NX:], "core", 1).astype(F32)

    def sum_of(rows):
        summed = rows[0]
        rows = rows.astype(BF16)
        for k in range(1, NX):
            summed = summed + from_peer(rows[k], "x", -k).astype(F32)
        return jnp.maximum(summed, 0.0).astype(BF16)

    def all_of(own):
        own = jnp.stack([own] + [from_peer(own, "x", k) for k in range(1, NX)])
        return jnp.concatenate([own, from_peer(own, "core", 1)], axis=0)

    rows_1, rows_2 = pair_of(x_1, 0), pair_of(x_2, 1)
    packed = all_of(sum_of(jnp.concatenate([rows_1, rows_2], axis=1)))
    out_1 = packed_down(at, packed, pos, down_weight, tokens, 0).reshape(NY, NZ, cut, width)
    out_2 = packed_down(at, packed, pos, down_weight, tokens, 1).reshape(NZ, NY, cut, width)
    out_1 = total(exchange(out_1, "y")).astype(BF16)
    out_2, out_1 = ring_total(out_2, "z", out_1)
    out_1 = total(exchange(out_1, "z")).astype(BF16)
    out_2 = out_2.astype(BF16)
    done = out_2[0].astype(F32)
    for k in range(1, NY):
        done = done + from_peer(out_2[k], "y", -k).astype(F32)
    out = jnp.concatenate([out_1, done.astype(BF16)], axis=0)
    whole = (activations, picks, up_weight, up_bias, down_weight)
    return lax.cond(room <= SLOTS, lambda: out, lambda: dense(*whole))


def solution(mesh):
    grid = Mesh(mesh.devices.reshape(NX, NC, NZ, NY), ("x", "core", "z", "y"))
    dp, clus = ("x", "core"), ("z", "y")
    placed = (P(clus, dp), P(), P(clus, dp, None), P(clus, None), P(clus, None, dp))
    return jax.shard_map(
        on_device, mesh=grid, in_specs=placed, out_specs=P(clus, dp), check_vma=False
    )
```

profile of v0, /device:TPU:8, one launch (start us, length us, event | category | flops | bytes accessed | tf_op | source)
XLA Modules:
  0.0 160.9 jit_solution(9090353226395814600)
XLA Ops:
  0.0 0.9 copy.121
  1.0 2.4 %collective-permute-start.5 = (bf16[16,1536]{1,0:T(8,128)(2,1)S(1)}, bf16[16,1536]{1,0:T(8,128)(2,1)S(1)}, u32[]{:S(2)}, u32[]{:S(2)}) collective-permute-start(bf16[16,1536]{1,0:T(8,128)(2,1)S(1)} %get-tuple-element.869), channel_id=1, source_target_pairs={{2,0},{3,1},{0,2},{1,3},{6,4},{7,5},{4,6},{5,7},{10,8},{11,9},{8,1... | collective-permute-start | bytes 147464 | tf_op jit(solution)/shard_map/ppermute | solution.py:35
  3.3 1.4 collective-permute-start.6
  4.7 0.7 collective-permute-start.4
  5.4 0.8 broadcast_in_dim.99
  6.1 8.5 %all-to-all-start = ((bf16[8,16,1536]{2,1,0:T(8,128)(2,1)}), bf16[8,16,1536]{2,1,0:T(8,128)(2,1)S(1)}, u32[]{:S(2)}, u32[]{:S(2)}) async-start(bf16[8,16,1536]{2,1,0:T(8,128)(2,1)} %broadcast_in_dim.99), calls=%async_computation | async-start | bytes 786432 | tf_op jit(solution)/shard_map/all_to_all | solution.py:20
  14.6 1.3 compare_reduce_fusion.1
  16.3 0.5 fusion.76
  17.8 0.9 convert_reduce_fusion
  18.8 1.1 convolution_reduce_fusion
  20.2 0.7 pad_maximum_fusion.2
  20.9 7.7 %all-to-all-done = bf16[8,16,1536]{2,1,0:T(8,128)(2,1)S(1)} async-done(((bf16[8,16,1536]{2,1,0:T(8,128)(2,1)}), bf16[8,16,1536]{2,1,0:T(8,128)(2,1)S(1)}, u32[]{:S(2)}, u32[]{:S(2)}) %all-to-all-start) | async-done | bytes 393248 | tf_op jit(solution)/shard_map/all_to_all | solution.py:20
  29.0 2.8 %collective-permute-start.7 = (bf16[4,16,1536]{2,1,0:T(8,128)(2,1)}, bf16[4,16,1536]{2,1,0:T(8,128)(2,1)}, u32[]{:S(2)}, u32[]{:S(2)}) collective-permute-start(bf16[4,16,1536]{2,1,0:T(8,128)(2,1)} %pad_maximum_fusion.2), channel_id=1, source_target_pairs={{4,0},{8,4},{12,8},{16,12},{20,16},{24,20},{28,24},{0,28},{5,1},{9... | collective-permute-start | bytes 589832 | tf_op jit(solution)/shard_map/ppermute | solution.py:35
  31.8 1.0 bitcast_dynamic-update-slice_fusion.10
  32.8 1.4 broadcast_in_dim.100
  34.2 6.1 %all-to-all-start.1 = ((bf16[4,8,16,1536]{3,2,1,0:T(8,128)(2,1)}), bf16[4,8,16,1536]{3,2,1,0:T(8,128)(2,1)S(1)}, u32[]{:S(2)}, u32[]{:S(2)}) async-start(bf16[4,8,16,1536]{3,2,1,0:T(8,128)(2,1)} %broadcast_in_dim.100), calls=%async_computation.1 | async-start | bytes 3145728 | tf_op jit(solution)/shard_map/all_to_all | solution.py:20
  40.3 3.2 %collective-permute-start.8 = (bf16[4,16,1536]{2,1,0:T(8,128)(2,1)}, bf16[4,16,1536]{2,1,0:T(8,128)(2,1)S(1)}, u32[]{:S(2)}, u32[]{:S(2)}) collective-permute-start(bf16[4,16,1536]{2,1,0:T(8,128)(2,1)} %collective-permute-done.7), channel_id=1, source_target_pairs={{4,0},{8,4},{12,8},{16,12},{20,16},{24,20},{28,24},{0,28},{5,1},{9... | collective-permute-start | bytes 589832 | tf_op jit(solution)/shard_map/ppermute | solution.py:35
  43.5 1.0 bitcast_dynamic-update-slice_fusion.9
  44.5 3.9 %collective-permute-done.11 = bf16[4,16,1536]{2,1,0:T(8,128)(2,1)S(1)} collective-permute-done((bf16[4,16,1536]{2,1,0:T(8,128)(2,1)}, bf16[4,16,1536]{2,1,0:T(8,128)(2,1)S(1)}, u32[]{:S(2)}, u32[]{:S(2)}) %collective-permute-start.11) | collective-permute-done | bytes 196640 | tf_op jit(solution)/shard_map/ppermute | solution.py:35
  48.4 3.5 %collective-permute-start.9 = (bf16[4,16,1536]{2,1,0:T(8,128)(2,1)S(1)}, bf16[4,16,1536]{2,1,0:T(8,128)(2,1)S(1)}, u32[]{:S(2)}, u32[]{:S(2)}) collective-permute-start(bf16[4,16,1536]{2,1,0:T(8,128)(2,1)S(1)} %collective-permute-done.8), channel_id=1, source_target_pairs={{4,0},{8,4},{12,8},{16,12},{20,16},{24,20},{28,24},{0,28},{5,1},{9... | collective-permute-start | bytes 589832 | tf_op jit(solution)/shard_map/ppermute | solution.py:35
  52.0 4.1 %collective-permute-done.9 = bf16[4,16,1536]{2,1,0:T(8,128)(2,1)S(1)} collective-permute-done((bf16[4,16,1536]{2,1,0:T(8,128)(2,1)S(1)}, bf16[4,16,1536]{2,1,0:T(8,128)(2,1)S(1)}, u32[]{:S(2)}, u32[]{:S(2)}) %collective-permute-start.9) | collective-permute-done | bytes 196640 | tf_op jit(solution)/shard_map/ppermute | solution.py:35
  56.1 0.7 copy-done.2
  56.7 0.9 slice.125
  57.6 3.7 %collective-permute-start.14 = (bf16[2,16,1536]{2,1,0:T(8,128)(2,1)S(1)}, bf16[2,16,1536]{2,1,0:T(8,128)(2,1)S(1)}, u32[]{:S(2)}, u32[]{:S(2)}) collective-permute-start(bf16[2,16,1536]{2,1,0:T(8,128)(2,1)S(1)} %slice.125), channel_id=1, source_target_pairs={{4,0},{8,4},{12,8},{16,12},{20,16},{24,20},{28,24},{0,28},{5,1},{9... | collective-permute-start | bytes 294920 | tf_op jit(solution)/shard_map/ppermute | solution.py:35
  61.3 1.0 slice.126
  62.7 6.0 %shard_map.57 = bf16[8,192,128]{2,1,0:T(8,128)(2,1)S(1)} custom-call(s32[8]{0:T(128)S(1)} %stack.97.at_ref, bf16[512,1536]{1,0:T(8,128)(2,1)S(1)} %bitcast.172, bf16[12,1536,128]{2,1,0:T(8,128)(2,1)} %w_ref.5, f32[3,4,128]{2,1,0:T(4,128)S(1)} %reshape.197.bias_ref, s32[3,16,256]{2,1,0:T(8,128)S(1)} %reshape.202.pos_ref), custom_call_target="tpu_custom_call" | custom-call | flops 4831838208 | bytes 9437184 | tf_op jit(solution)/shard_map/pallas_call | solution.py:99
  68.8 0.9 bitcast_dynamic-update-slice_fusion.6
  69.8 0.9 bitcast_dynamic-update-slice_fusion.4
  70.8 4.4 %shard_map.58 = bf16[8,192,128]{2,1,0:T(8,128)(2,1)S(1)} custom-call(s32[8]{0:T(128)S(1)} %stack.97.at_ref, bf16[512,1536]{1,0:T(8,128)(2,1)S(1)} %bitcast.173, bf16[12,1536,128]{2,1,0:T(8,128)(2,1)S(1)} %bitcast.183, f32[3,4,128]{2,1,0:T(4,128)S(1)} %reshape.197.bias_ref, s32[3,16,256]{2,1,0:T(8,128)S(1)} %reshape.202.pos_ref), custom_call_target="tpu_custom_call" | custom-call | flops 4831838208 | bytes 9437184 | tf_op jit(solution)/shard_map/pallas_call | solution.py:99
  75.2 0.6 collective-permute-start.16
  75.8 1.0 collective-permute-done.16
  77.0 1.6 collective-permute-start.17
  78.5 2.7 %collective-permute-start.18 = (bf16[384,128]{1,0:T(8,128)(2,1)S(1)}, bf16[384,128]{1,0:T(8,128)(2,1)S(1)}, u32[]{:S(2)}, u32[]{:S(2)}) collective-permute-start(bf16[384,128]{1,0:T(8,128)(2,1)S(1)} %get-tuple-element.861), channel_id=1, source_target_pairs={{128,0},{192,64},{0,128},{64,192},{129,1},{193,65},{1,129},{65,193... | collective-permute-start | bytes 294920 | tf_op jit(solution)/shard_map/ppermute | solution.py:35
  81.3 1.4 collective-permute-start.19
  82.7 0.6 collective-permute-done.17
  83.3 3.1 %collective-permute-done.18 = bf16[384,128]{1,0:T(8,128)(2,1)S(1)} collective-permute-done((bf16[384,128]{1,0:T(8,128)(2,1)S(1)}, bf16[384,128]{1,0:T(8,128)(2,1)S(1)}, u32[]{:S(2)}, u32[]{:S(2)}) %collective-permute-start.18) | collective-permute-done | bytes 98336 | tf_op jit(solution)/shard_map/ppermute | solution.py:35
  86.5 2.4 %collective-permute-start.20 = (bf16[384,128]{1,0:T(8,128)(2,1)S(1)}, bf16[384,128]{1,0:T(8,128)(2,1)S(1)}, u32[]{:S(2)}, u32[]{:S(2)}) collective-permute-start(bf16[384,128]{1,0:T(8,128)(2,1)S(1)} %get-tuple-element.847), channel_id=1, source_target_pairs={{64,0},{128,64},{192,128},{0,192},{65,1},{129,65},{193,129},{1,193... | collective-permute-start | bytes 294920 | tf_op jit(solution)/shard_map/ppermute | solution.py:35
  88.8 1.1 collective-permute-start.21
  90.0 0.7 collective-permute-start.22
  90.6 2.1 %collective-permute-done.20 = bf16[384,128]{1,0:T(8,128)(2,1)S(1)} collective-permute-done((bf16[384,128]{1,0:T(8,128)(2,1)S(1)}, bf16[384,128]{1,0:T(8,128)(2,1)S(1)}, u32[]{:S(2)}, u32[]{:S(2)}) %collective-permute-start.20) | collective-permute-done | bytes 98336 | tf_op jit(solution)/shard_map/ppermute | solution.py:35
  92.7 2.3 %collective-permute-done.21 = bf16[384,128]{1,0:T(8,128)(2,1)S(1)} collective-permute-done((bf16[384,128]{1,0:T(8,128)(2,1)S(1)}, bf16[384,128]{1,0:T(8,128)(2,1)S(1)}, u32[]{:S(2)}, u32[]{:S(2)}) %collective-permute-start.21) | collective-permute-done | bytes 98336 | tf_op jit(solution)/shard_map/ppermute | solution.py:35
  95.0 1.0 collective-permute-done.22
  96.3 1.6 %collective-permute-done.23 = bf16[4,384,128]{2,1,0:T(8,128)(2,1)S(1)} collective-permute-done((bf16[4,384,128]{2,1,0:T(8,128)(2,1)S(1)}, bf16[4,384,128]{2,1,0:T(8,128)(2,1)S(1)}, u32[]{:S(2)}, u32[]{:S(2)}) %collective-permute-start.23) | collective-permute-done | bytes 393248 | tf_op jit(solution)/shard_map/ppermute | solution.py:35
  98.0 6.6 %shard_map.59 = bf16[512,1536]{1,0:T(8,128)(2,1)S(1)} custom-call(s32[8]{0:T(128)S(1)} %stack.97.at_ref, bf16[8,384,128]{2,1,0:T(8,128)(2,1)S(1)} %constant_dynamic-update-slice_fusion.2.packed_ref, s32[3,16,256]{2,1,0:T(8,128)S(1)} %reshape.202.pos_ref, bf16[12,128,1536]{2,1,0:T(8,128)(2,1)S(1)} %bitcast.185), custom_call_target="tpu_custom_call" | custom-call | flops 2415919104 | bytes 7340032 | tf_op jit(solution)/shard_map/pallas_call | solution.py:147
  104.6 0.7 fusion.74
  105.4 7.3 %shard_map.60 = bf16[512,1536]{1,0:T(8,128)(2,1)} custom-call(s32[8]{0:T(128)S(1)} %stack.97.at_ref, bf16[8,384,128]{2,1,0:T(8,128)(2,1)S(1)} %constant_dynamic-update-slice_fusion.2.packed_ref, s32[3,16,256]{2,1,0:T(8,128)S(1)} %reshape.202.pos_ref, bf16[12,128,1536]{2,1,0:T(8,128)(2,1)S(1)} %bitcast.185), custom_call_target="tpu_custom_call" | custom-call | flops 2415919104 | bytes 7340032 | tf_op jit(solution)/shard_map/pallas_call | solution.py:147
  112.8 4.6 %all-to-all-start.2 = ((bf16[4,8,16,1536]{3,2,1,0:T(8,128)(2,1)}), bf16[4,8,16,1536]{3,2,1,0:T(8,128)(2,1)S(1)}, u32[]{:S(2)}, u32[]{:S(2)}) async-start(bf16[4,8,16,1536]{3,2,1,0:T(8,128)(2,1)} %bitcast.55), calls=%async_computation.2 | async-start | bytes 3145728 | tf_op jit(solution)/shard_map/all_to_all | solution.py:26
  117.4 3.2 %collective-permute-start.24 = (bf16[2,16,1536]{2,1,0:T(8,128)(2,1)}, bf16[2,16,1536]{2,1,0:T(8,128)(2,1)S(1)}, u32[]{:S(2)}, u32[]{:S(2)}) collective-permute-start(bf16[2,16,1536]{2,1,0:T(8,128)(2,1)} %bitcast.48), channel_id=1, source_target_pairs={{4,0},{8,4},{12,8},{16,12},{20,16},{24,20},{28,24},{0,28},{5,1},{9... | collective-permute-start | bytes 294920 | tf_op jit(solution)/shard_map/ppermute | solution.py:35
  121.0 2.2 %collective-permute-done.24 = bf16[2,16,1536]{2,1,0:T(8,128)(2,1)S(1)} collective-permute-done((bf16[2,16,1536]{2,1,0:T(8,128)(2,1)}, bf16[2,16,1536]{2,1,0:T(8,128)(2,1)S(1)}, u32[]{:S(2)}, u32[]{:S(2)}) %collective-permute-start.24) | collective-permute-done | bytes 98336 | tf_op jit(solution)/shard_map/ppermute | solution.py:35
  123.2 3.6 %collective-permute-start.25 = (bf16[4,16,1536]{2,1,0:T(8,128)(2,1)S(1)}, bf16[4,16,1536]{2,1,0:T(8,128)(2,1)S(1)}, u32[]{:S(2)}, u32[]{:S(2)}) collective-permute-start(bf16[4,16,1536]{2,1,0:T(8,128)(2,1)S(1)} %pad_maximum_fusion.3), channel_id=1, source_target_pairs={{4,0},{8,4},{12,8},{16,12},{20,16},{24,20},{28,24},{0,28},{5,1},{9... | collective-permute-start | bytes 589832 | tf_op jit(solution)/shard_map/ppermute | solution.py:35
  126.8 1.4 collective-permute-done.28
  128.3 1.6 %collective-permute-done.25 = bf16[4,16,1536]{2,1,0:T(8,128)(2,1)S(1)} collective-permute-done((bf16[4,16,1536]{2,1,0:T(8,128)(2,1)S(1)}, bf16[4,16,1536]{2,1,0:T(8,128)(2,1)S(1)}, u32[]{:S(2)}, u32[]{:S(2)}) %collective-permute-start.25) | collective-permute-done | bytes 196640 | tf_op jit(solution)/shard_map/ppermute | solution.py:35
  130.0 3.8 %collective-permute-start.26 = (bf16[4,16,1536]{2,1,0:T(8,128)(2,1)S(1)}, bf16[4,16,1536]{2,1,0:T(8,128)(2,1)S(1)}, u32[]{:S(2)}, u32[]{:S(2)}) collective-permute-start(bf16[4,16,1536]{2,1,0:T(8,128)(2,1)S(1)} %fusion.12), channel_id=1, source_target_pairs={{4,0},{8,4},{12,8},{16,12},{20,16},{24,20},{28,24},{0,28},{5,1},{9... | collective-permute-start | bytes 589832 | tf_op jit(solution)/shard_map/ppermute | solution.py:35
  133.8 1.4 collective-permute-done.29
  135.2 1.7 %collective-permute-done.26 = bf16[4,16,1536]{2,1,0:T(8,128)(2,1)S(1)} collective-permute-done((bf16[4,16,1536]{2,1,0:T(8,128)(2,1)S(1)}, bf16[4,16,1536]{2,1,0:T(8,128)(2,1)S(1)}, u32[]{:S(2)}, u32[]{:S(2)}) %collective-permute-start.26) | collective-permute-done | bytes 196640 | tf_op jit(solution)/shard_map/ppermute | solution.py:35
  137.0 1.1 reduce_sum.47
  138.1 3.7 %collective-permute-start.30 = (bf16[4,16,1536]{2,1,0:T(8,128)(2,1)S(1)}, bf16[4,16,1536]{2,1,0:T(8,128)(2,1)S(1)}, u32[]{:S(2)}, u32[]{:S(2)}) collective-permute-start(bf16[4,16,1536]{2,1,0:T(8,128)(2,1)S(1)} %fusion.13), channel_id=1, source_target_pairs={{4,0},{8,4},{12,8},{16,12},{20,16},{24,20},{28,24},{0,28},{5,1},{9... | collective-permute-start | bytes 589832 | tf_op jit(solution)/shard_map/ppermute | solution.py:35
  141.8 4.5 %all-to-all-start.3 = ((bf16[8,16,1536]{2,1,0:T(8,128)(2,1)}), bf16[8,16,1536]{2,1,0:T(8,128)(2,1)S(1)}, u32[]{:S(2)}, u32[]{:S(2)}) async-start(bf16[8,16,1536]{2,1,0:T(8,128)(2,1)} %reduce_sum.47), calls=%async_computation.3 | async-start | bytes 786432 | tf_op jit(solution)/shard_map/all_to_all | solution.py:26
  146.3 4.9 %collective-permute-done.31 = bf16[4,16,1536]{2,1,0:T(8,128)(2,1)S(1)} collective-permute-done((bf16[4,16,1536]{2,1,0:T(8,128)(2,1)S(1)}, bf16[4,16,1536]{2,1,0:T(8,128)(2,1)S(1)}, u32[]{:S(2)}, u32[]{:S(2)}) %collective-permute-start.31) | collective-permute-done | bytes 196640 | tf_op jit(solution)/shard_map/ppermute | solution.py:35
  151.3 2.4 %collective-permute-start.32 = (bf16[16,1536]{1,0:T(8,128)(2,1)S(1)}, bf16[16,1536]{1,0:T(8,128)(2,1)S(1)}, u32[]{:S(2)}, u32[]{:S(2)}) collective-permute-start(bf16[16,1536]{1,0:T(8,128)(2,1)S(1)} %get-tuple-element.862), channel_id=1, source_target_pairs={{3,0},{0,1},{1,2},{2,3},{7,4},{4,5},{5,6},{6,7},{11,8},{8,9},{9,10... | collective-permute-start | bytes 147464 | tf_op jit(solution)/shard_map/ppermute | solution.py:35
  153.7 2.1 %collective-permute-start.33 = (bf16[16,1536]{1,0:T(8,128)(2,1)S(1)}, bf16[16,1536]{1,0:T(8,128)(2,1)S(1)}, u32[]{:S(2)}, u32[]{:S(2)}) collective-permute-start(bf16[16,1536]{1,0:T(8,128)(2,1)S(1)} %get-tuple-element.864), channel_id=1, source_target_pairs={{2,0},{3,1},{0,2},{1,3},{6,4},{7,5},{4,6},{5,7},{10,8},{11,9},{8,1... | collective-permute-start | bytes 147464 | tf_op jit(solution)/shard_map/ppermute | solution.py:35
  155.8 2.5 %collective-permute-start.34 = (bf16[16,1536]{1,0:T(8,128)(2,1)S(1)}, bf16[16,1536]{1,0:T(8,128)(2,1)S(1)}, u32[]{:S(2)}, u32[]{:S(2)}) collective-permute-start(bf16[16,1536]{1,0:T(8,128)(2,1)S(1)} %get-tuple-element.863), channel_id=1, source_target_pairs={{1,0},{2,1},{3,2},{0,3},{5,4},{6,5},{7,6},{4,7},{9,8},{10,9},{11,1... | collective-permute-start | bytes 147464 | tf_op jit(solution)/shard_map/ppermute | solution.py:35
  159.3 0.8 collective-permute-done.34
  160.2 0.6 pad_maximum_fusion.5
  (99 shorter events, 4.4 us)
Async XLA Ops:
  0.0 17.6 %copy-start.1 = (s32[1024,48]{0,1:T(8,128)S(1)}, s32[1024,48]{0,1:T(8,128)}, u32[]{:S(2)}) copy-start(s32[1024,48]{0,1:T(8,128)} %param.18) | copy-start | bytes 589828
  0.0 18.7 %copy-start.5 = (f32[12,128]{1,0:T(8,128)S(1)}, f32[12,128]{1,0:T(8,128)}, u32[]{:S(2)}) copy-start(f32[12,128]{1,0:T(8,128)} %param.20) | copy-start | bytes 18436
  1.0 19.2 %collective-permute-start.5 = (bf16[16,1536]{1,0:T(8,128)(2,1)S(1)}, bf16[16,1536]{1,0:T(8,128)(2,1)S(1)}, u32[]{:S(2)}, u32[]{:S(2)}) collective-permute-start(bf16[16,1536]{1,0:T(8,128)(2,1)S(1)} %get-tuple-element.869), channel_id=1, source_target_pairs={{2,0},{3,1},{0,2},{1,3},{6,4},{7,5},{4,6},{5,7},{10,8},{11,9},{8,1... | collective-permute-start | bytes 147464 | tf_op jit(solution)/shard_map/ppermute | solution.py:35
  3.3 16.8 %collective-permute-start.6 = (bf16[16,1536]{1,0:T(8,128)(2,1)S(1)}, bf16[16,1536]{1,0:T(8,128)(2,1)S(1)}, u32[]{:S(2)}, u32[]{:S(2)}) collective-permute-start(bf16[16,1536]{1,0:T(8,128)(2,1)S(1)} %get-tuple-element.869), channel_id=1, source_target_pairs={{3,0},{0,1},{1,2},{2,3},{7,4},{4,5},{5,6},{6,7},{11,8},{8,9},{9,10... | collective-permute-start | bytes 147464 | tf_op jit(solution)/shard_map/ppermute | solution.py:35
  4.7 15.5 %collective-permute-start.4 = (bf16[16,1536]{1,0:T(8,128)(2,1)S(1)}, bf16[16,1536]{1,0:T(8,128)(2,1)S(1)}, u32[]{:S(2)}, u32[]{:S(2)}) collective-permute-start(bf16[16,1536]{1,0:T(8,128)(2,1)S(1)} %get-tuple-element.869), channel_id=1, source_target_pairs={{1,0},{2,1},{3,2},{0,3},{5,4},{6,5},{7,6},{4,7},{9,8},{10,9},{11,1... | collective-permute-start | bytes 147464 | tf_op jit(solution)/shard_map/ppermute | solution.py:35
  6.1 22.4 %all-to-all-start = ((bf16[8,16,1536]{2,1,0:T(8,128)(2,1)}), bf16[8,16,1536]{2,1,0:T(8,128)(2,1)S(1)}, u32[]{:S(2)}, u32[]{:S(2)}) async-start(bf16[8,16,1536]{2,1,0:T(8,128)(2,1)} %broadcast_in_dim.99), calls=%async_computation | async-start | bytes 786432 | tf_op jit(solution)/shard_map/all_to_all | solution.py:20
  28.6 11.7 %collective-permute-start.10 = (bf16[4,16,1536]{2,1,0:T(8,128)(2,1)}, bf16[4,16,1536]{2,1,0:T(8,128)(2,1)}, u32[]{:S(2)}, u32[]{:S(2)}) collective-permute-start(bf16[4,16,1536]{2,1,0:T(8,128)(2,1)} %pad_maximum_fusion.2), channel_id=1, source_target_pairs={{28,0},{0,4},{4,8},{8,12},{12,16},{16,20},{20,24},{24,28},{29,1},{... | collective-permute-start | bytes 589832 | tf_op jit(solution)/shard_map/ppermute | solution.py:35
  29.0 11.2 %collective-permute-start.7 = (bf16[4,16,1536]{2,1,0:T(8,128)(2,1)}, bf16[4,16,1536]{2,1,0:T(8,128)(2,1)}, u32[]{:S(2)}, u32[]{:S(2)}) collective-permute-start(bf16[4,16,1536]{2,1,0:T(8,128)(2,1)} %pad_maximum_fusion.2), channel_id=1, source_target_pairs={{4,0},{8,4},{12,8},{16,12},{20,16},{24,20},{28,24},{0,28},{5,1},{9... | collective-permute-start | bytes 589832 | tf_op jit(solution)/shard_map/ppermute | solution.py:35
  34.2 22.6 %all-to-all-start.1 = ((bf16[4,8,16,1536]{3,2,1,0:T(8,128)(2,1)}), bf16[4,8,16,1536]{3,2,1,0:T(8,128)(2,1)S(1)}, u32[]{:S(2)}, u32[]{:S(2)}) async-start(bf16[4,8,16,1536]{3,2,1,0:T(8,128)(2,1)} %broadcast_in_dim.100), calls=%async_computation.1 | async-start | bytes 3145728 | tf_op jit(solution)/shard_map/all_to_all | solution.py:20
  40.2 8.1 %collective-permute-start.11 = (bf16[4,16,1536]{2,1,0:T(8,128)(2,1)}, bf16[4,16,1536]{2,1,0:T(8,128)(2,1)S(1)}, u32[]{:S(2)}, u32[]{:S(2)}) collective-permute-start(bf16[4,16,1536]{2,1,0:T(8,128)(2,1)} %collective-permute-done.10), channel_id=1, source_target_pairs={{28,0},{0,4},{4,8},{8,12},{12,16},{16,20},{20,24},{24,28},{29,1},{... | collective-permute-start | bytes 589832 | tf_op jit(solution)/shard_map/ppermute | solution.py:35
  40.3 8.1 %collective-permute-start.8 = (bf16[4,16,1536]{2,1,0:T(8,128)(2,1)}, bf16[4,16,1536]{2,1,0:T(8,128)(2,1)S(1)}, u32[]{:S(2)}, u32[]{:S(2)}) collective-permute-start(bf16[4,16,1536]{2,1,0:T(8,128)(2,1)} %collective-permute-done.7), channel_id=1, source_target_pairs={{4,0},{8,4},{12,8},{16,12},{20,16},{24,20},{28,24},{0,28},{5,1},{9... | collective-permute-start | bytes 589832 | tf_op jit(solution)/shard_map/ppermute | solution.py:35
  48.4 7.7 %copy-start.3 = (bf16[4,16,1536]{2,1,0:T(8,128)(2,1)}, bf16[4,16,1536]{2,1,0:T(8,128)(2,1)S(1)}, u32[]{:S(2)}) copy-start(bf16[4,16,1536]{2,1,0:T(8,128)(2,1)S(1)} %collective-permute-done.11) | copy-start | bytes 589828
  48.4 8.3 %collective-permute-start.12 = (bf16[4,16,1536]{2,1,0:T(8,128)(2,1)S(1)}, bf16[4,16,1536]{2,1,0:T(8,128)(2,1)}, u32[]{:S(2)}, u32[]{:S(2)}) collective-permute-start(bf16[4,16,1536]{2,1,0:T(8,128)(2,1)S(1)} %collective-permute-done.11), channel_id=1, source_target_pairs={{28,0},{0,4},{4,8},{8,12},{12,16},{16,20},{20,24},{24,28},{29,1},{... | collective-permute-start | bytes 589832 | tf_op jit(solution)/shard_map/ppermute | solution.py:35
  48.4 7.6 %collective-permute-start.9 = (bf16[4,16,1536]{2,1,0:T(8,128)(2,1)S(1)}, bf16[4,16,1536]{2,1,0:T(8,128)(2,1)S(1)}, u32[]{:S(2)}, u32[]{:S(2)}) collective-permute-start(bf16[4,16,1536]{2,1,0:T(8,128)(2,1)S(1)} %collective-permute-done.8), channel_id=1, source_target_pairs={{4,0},{8,4},{12,8},{16,12},{20,16},{24,20},{28,24},{0,28},{5,1},{9... | collective-permute-start | bytes 589832 | tf_op jit(solution)/shard_map/ppermute | solution.py:35
  56.0 0.7 copy-start.2
  57.6 11.2 %collective-permute-start.14 = (bf16[2,16,1536]{2,1,0:T(8,128)(2,1)S(1)}, bf16[2,16,1536]{2,1,0:T(8,128)(2,1)S(1)}, u32[]{:S(2)}, u32[]{:S(2)}) collective-permute-start(bf16[2,16,1536]{2,1,0:T(8,128)(2,1)S(1)} %slice.125), channel_id=1, source_target_pairs={{4,0},{8,4},{12,8},{16,12},{20,16},{24,20},{28,24},{0,28},{5,1},{9... | collective-permute-start | bytes 294920 | tf_op jit(solution)/shard_map/ppermute | solution.py:35
  61.3 9.5 %slice-start = ((s8[4718592]{0:T(1024)(128)(4,1)}), s8[4194304]{0:T(1024)(128)(4,1)S(1)}, s32[]{:S(2)}) async-start(s8[4718592]{0:T(1024)(128)(4,1)} %bitcast.182), calls=%async_computation.4 | async-start | bytes 8388608
  62.4 7.4 %copy-start.4 = (bf16[4,16,1536]{2,1,0:T(8,128)(2,1)S(1)}, bf16[4,16,1536]{2,1,0:T(8,128)(2,1)}, u32[]{:S(2)}) copy-start(bf16[4,16,1536]{2,1,0:T(8,128)(2,1)} %copy-done.3) | copy-start | bytes 589828
  62.4 8.4 %slice-start.1 = ((s8[4718592]{0:T(1024)(128)(4,1)}), s8[524288]{0:T(1024)(128)(4,1)S(1)}, s32[]{:S(2)}) async-start(s8[4718592]{0:T(1024)(128)(4,1)} %bitcast.182), calls=%async_computation.5 | async-start | bytes 1048576
  62.4 6.4 %collective-permute-start.15 = (bf16[2,16,1536]{2,1,0:T(8,128)(2,1)S(1)}, bf16[2,16,1536]{2,1,0:T(8,128)(2,1)S(1)}, u32[]{:S(2)}, u32[]{:S(2)}) collective-permute-start(bf16[2,16,1536]{2,1,0:T(8,128)(2,1)S(1)} %slice.126), channel_id=1, source_target_pairs={{28,0},{0,4},{4,8},{8,12},{12,16},{16,20},{20,24},{24,28},{29,1},{... | collective-permute-start | bytes 294920 | tf_op jit(solution)/shard_map/ppermute | solution.py:35
  68.7 7.1 %collective-permute-start.13 = (bf16[4,192,128]{2,1,0:T(8,128)(2,1)S(1)}, bf16[4,192,128]{2,1,0:T(8,128)(2,1)S(1)}, u32[]{:S(2)}, u32[]{:S(2)}) collective-permute-start(bf16[4,192,128]{2,1,0:T(8,128)(2,1)S(1)} %slice.155), channel_id=1, source_target_pairs={{32,0},{0,32},{33,1},{1,33},{34,2},{2,34},{35,3},{3,35},{36,4},{4,... | collective-permute-start | bytes 589832 | tf_op jit(solution)/shard_map/ppermute | solution.py:35
  70.8 27.2 %slice-start.2 = ((s8[4718592]{0:T(1024)(128)(4,1)}), s8[4194304]{0:T(1024)(128)(4,1)S(1)}, s32[]{:S(2)}) async-start(s8[4718592]{0:T(1024)(128)(4,1)} %bitcast.184), calls=%async_computation.6 | async-start | bytes 8388608
  70.8 27.2 %slice-start.3 = ((s8[4718592]{0:T(1024)(128)(4,1)}), s8[524288]{0:T(1024)(128)(4,1)S(1)}, s32[]{:S(2)}) async-start(s8[4718592]{0:T(1024)(128)(4,1)} %bitcast.184), calls=%async_computation.7 | async-start | bytes 1048576
  75.2 1.6 %collective-permute-start.16 = (bf16[4,192,128]{2,1,0:T(8,128)(2,1)S(1)}, bf16[4,192,128]{2,1,0:T(8,128)(2,1)S(1)}, u32[]{:S(2)}, u32[]{:S(2)}) collective-permute-start(bf16[4,192,128]{2,1,0:T(8,128)(2,1)S(1)} %slice.157), channel_id=1, source_target_pairs={{32,0},{0,32},{33,1},{1,33},{34,2},{2,34},{35,3},{3,35},{36,4},{4,... | collective-permute-start | bytes 589832 | tf_op jit(solution)/shard_map/ppermute | solution.py:35
  77.0 6.4 %collective-permute-start.17 = (bf16[384,128]{1,0:T(8,128)(2,1)S(1)}, bf16[384,128]{1,0:T(8,128)(2,1)S(1)}, u32[]{:S(2)}, u32[]{:S(2)}) collective-permute-start(bf16[384,128]{1,0:T(8,128)(2,1)S(1)} %get-tuple-element.859), channel_id=1, source_target_pairs={{192,0},{0,64},{64,128},{128,192},{193,1},{1,65},{65,129},{129,193... | collective-permute-start | bytes 294920 | tf_op jit(solution)/shard_map/ppermute | solution.py:35
  78.5 7.9 %collective-permute-start.18 = (bf16[384,128]{1,0:T(8,128)(2,1)S(1)}, bf16[384,128]{1,0:T(8,128)(2,1)S(1)}, u32[]{:S(2)}, u32[]{:S(2)}) collective-permute-start(bf16[384,128]{1,0:T(8,128)(2,1)S(1)} %get-tuple-element.861), channel_id=1, source_target_pairs={{128,0},{192,64},{0,128},{64,192},{129,1},{193,65},{1,129},{65,193... | collective-permute-start | bytes 294920 | tf_op jit(solution)/shard_map/ppermute | solution.py:35
  81.3 5.1 %collective-permute-start.19 = (bf16[384,128]{1,0:T(8,128)(2,1)S(1)}, bf16[384,128]{1,0:T(8,128)(2,1)S(1)}, u32[]{:S(2)}, u32[]{:S(2)}) collective-permute-start(bf16[384,128]{1,0:T(8,128)(2,1)S(1)} %get-tuple-element.860), channel_id=1, source_target_pairs={{64,0},{128,64},{192,128},{0,192},{65,1},{129,65},{193,129},{1,193... | collective-permute-start | bytes 294920 | tf_op jit(solution)/shard_map/ppermute | solution.py:35
  86.5 6.2 %collective-permute-start.20 = (bf16[384,128]{1,0:T(8,128)(2,1)S(1)}, bf16[384,128]{1,0:T(8,128)(2,1)S(1)}, u32[]{:S(2)}, u32[]{:S(2)}) collective-permute-start(bf16[384,128]{1,0:T(8,128)(2,1)S(1)} %get-tuple-element.847), channel_id=1, source_target_pairs={{64,0},{128,64},{192,128},{0,192},{65,1},{129,65},{193,129},{1,193... | collective-permute-start | bytes 294920 | tf_op jit(solution)/shard_map/ppermute | solution.py:35
  88.8 6.2 %collective-permute-start.21 = (bf16[384,128]{1,0:T(8,128)(2,1)S(1)}, bf16[384,128]{1,0:T(8,128)(2,1)S(1)}, u32[]{:S(2)}, u32[]{:S(2)}) collective-permute-start(bf16[384,128]{1,0:T(8,128)(2,1)S(1)} %get-tuple-element.847), channel_id=1, source_target_pairs={{128,0},{192,64},{0,128},{64,192},{129,1},{193,65},{1,129},{65,193... | collective-permute-start | bytes 294920 | tf_op jit(solution)/shard_map/ppermute | solution.py:35
  90.0 6.1 %collective-permute-start.22 = (bf16[384,128]{1,0:T(8,128)(2,1)S(1)}, bf16[384,128]{1,0:T(8,128)(2,1)S(1)}, u32[]{:S(2)}, u32[]{:S(2)}) collective-permute-start(bf16[384,128]{1,0:T(8,128)(2,1)S(1)} %get-tuple-element.847), channel_id=1, source_target_pairs={{192,0},{0,64},{64,128},{128,192},{193,1},{1,65},{65,129},{129,193... | collective-permute-start | bytes 294920 | tf_op jit(solution)/shard_map/ppermute | solution.py:35
  96.1 1.8 %collective-permute-start.23 = (bf16[4,384,128]{2,1,0:T(8,128)(2,1)S(1)}, bf16[4,384,128]{2,1,0:T(8,128)(2,1)S(1)}, u32[]{:S(2)}, u32[]{:S(2)}) collective-permute-start(bf16[4,384,128]{2,1,0:T(8,128)(2,1)S(1)} %pad_maximum_fusion.1), channel_id=1, source_target_pairs={{32,0},{0,32},{33,1},{1,33},{34,2},{2,34},{35,3},{3,35},{36,4},{4,... | collective-permute-start | bytes 1179656 | tf_op jit(solution)/shard_map/ppermute | solution.py:35
  105.3 15.2 %collective-permute-start.27 = (bf16[2,16,1536]{2,1,0:T(8,128)(2,1)S(1)}, bf16[2,16,1536]{2,1,0:T(8,128)(2,1)S(1)}, u32[]{:S(2)}, u32[]{:S(2)}) collective-permute-start(bf16[2,16,1536]{2,1,0:T(8,128)(2,1)S(1)} %bitcast.200), channel_id=1, source_target_pairs={{28,0},{0,4},{4,8},{8,12},{12,16},{16,20},{20,24},{24,28},{29,1},{... | collective-permute-start | bytes 294920 | tf_op jit(solution)/shard_map/ppermute | solution.py:35
  112.8 24.3 %all-to-all-start.2 = ((bf16[4,8,16,1536]{3,2,1,0:T(8,128)(2,1)}), bf16[4,8,16,1536]{3,2,1,0:T(8,128)(2,1)S(1)}, u32[]{:S(2)}, u32[]{:S(2)}) async-start(bf16[4,8,16,1536]{3,2,1,0:T(8,128)(2,1)} %bitcast.55), calls=%async_computation.2 | async-start | bytes 3145728 | tf_op jit(solution)/shard_map/all_to_all | solution.py:26
  117.4 5.8 %collective-permute-start.24 = (bf16[2,16,1536]{2,1,0:T(8,128)(2,1)}, bf16[2,16,1536]{2,1,0:T(8,128)(2,1)S(1)}, u32[]{:S(2)}, u32[]{:S(2)}) collective-permute-start(bf16[2,16,1536]{2,1,0:T(8,128)(2,1)} %bitcast.48), channel_id=1, source_target_pairs={{4,0},{8,4},{12,8},{16,12},{20,16},{24,20},{28,24},{0,28},{5,1},{9... | collective-permute-start | bytes 294920 | tf_op jit(solution)/shard_map/ppermute | solution.py:35
  120.7 7.5 %collective-permute-start.28 = (bf16[4,16,1536]{2,1,0:T(8,128)(2,1)S(1)}, bf16[4,16,1536]{2,1,0:T(8,128)(2,1)S(1)}, u32[]{:S(2)}, u32[]{:S(2)}) collective-permute-start(bf16[4,16,1536]{2,1,0:T(8,128)(2,1)S(1)} %pad_maximum_fusion.4), channel_id=1, source_target_pairs={{28,0},{0,4},{4,8},{8,12},{12,16},{16,20},{20,24},{24,28},{29,1},{... | collective-permute-start | bytes 589832 | tf_op jit(solution)/shard_map/ppermute | solution.py:35
  123.2 6.8 %collective-permute-start.25 = (bf16[4,16,1536]{2,1,0:T(8,128)(2,1)S(1)}, bf16[4,16,1536]{2,1,0:T(8,128)(2,1)S(1)}, u32[]{:S(2)}, u32[]{:S(2)}) collective-permute-start(bf16[4,16,1536]{2,1,0:T(8,128)(2,1)S(1)} %pad_maximum_fusion.3), channel_id=1, source_target_pairs={{4,0},{8,4},{12,8},{16,12},{20,16},{24,20},{28,24},{0,28},{5,1},{9... | collective-permute-start | bytes 589832 | tf_op jit(solution)/shard_map/ppermute | solution.py:35
  128.2 7.0 %collective-permute-start.29 = (bf16[4,16,1536]{2,1,0:T(8,128)(2,1)S(1)}, bf16[4,16,1536]{2,1,0:T(8,128)(2,1)S(1)}, u32[]{:S(2)}, u32[]{:S(2)}) collective-permute-start(bf16[4,16,1536]{2,1,0:T(8,128)(2,1)S(1)} %fusion.10), channel_id=1, source_target_pairs={{28,0},{0,4},{4,8},{8,12},{12,16},{16,20},{20,24},{24,28},{29,1},{... | collective-permute-start | bytes 589832 | tf_op jit(solution)/shard_map/ppermute | solution.py:35
  130.0 7.0 %collective-permute-start.26 = (bf16[4,16,1536]{2,1,0:T(8,128)(2,1)S(1)}, bf16[4,16,1536]{2,1,0:T(8,128)(2,1)S(1)}, u32[]{:S(2)}, u32[]{:S(2)}) collective-permute-start(bf16[4,16,1536]{2,1,0:T(8,128)(2,1)S(1)} %fusion.12), channel_id=1, source_target_pairs={{4,0},{8,4},{12,8},{16,12},{20,16},{24,20},{28,24},{0,28},{5,1},{9... | collective-permute-start | bytes 589832 | tf_op jit(solution)/shard_map/ppermute | solution.py:35
  138.1 8.2 %collective-permute-start.30 = (bf16[4,16,1536]{2,1,0:T(8,128)(2,1)S(1)}, bf16[4,16,1536]{2,1,0:T(8,128)(2,1)S(1)}, u32[]{:S(2)}, u32[]{:S(2)}) collective-permute-start(bf16[4,16,1536]{2,1,0:T(8,128)(2,1)S(1)} %fusion.13), channel_id=1, source_target_pairs={{4,0},{8,4},{12,8},{16,12},{20,16},{24,20},{28,24},{0,28},{5,1},{9... | collective-permute-start | bytes 589832 | tf_op jit(solution)/shard_map/ppermute | solution.py:35
  141.8 9.4 %collective-permute-start.31 = (bf16[4,16,1536]{2,1,0:T(8,128)(2,1)S(1)}, bf16[4,16,1536]{2,1,0:T(8,128)(2,1)S(1)}, u32[]{:S(2)}, u32[]{:S(2)}) collective-permute-start(bf16[4,16,1536]{2,1,0:T(8,128)(2,1)S(1)} %fusion.11), channel_id=1, source_target_pairs={{28,0},{0,4},{4,8},{8,12},{12,16},{16,20},{20,24},{24,28},{29,1},{... | collective-permute-start | bytes 589832 | tf_op jit(solution)/shard_map/ppermute | solution.py:35
  141.8 18.3 %all-to-all-start.3 = ((bf16[8,16,1536]{2,1,0:T(8,128)(2,1)}), bf16[8,16,1536]{2,1,0:T(8,128)(2,1)S(1)}, u32[]{:S(2)}, u32[]{:S(2)}) async-start(bf16[8,16,1536]{2,1,0:T(8,128)(2,1)} %reduce_sum.47), calls=%async_computation.3 | async-start | bytes 786432 | tf_op jit(solution)/shard_map/all_to_all | solution.py:26
  151.3 7.7 %collective-permute-start.32 = (bf16[16,1536]{1,0:T(8,128)(2,1)S(1)}, bf16[16,1536]{1,0:T(8,128)(2,1)S(1)}, u32[]{:S(2)}, u32[]{:S(2)}) collective-permute-start(bf16[16,1536]{1,0:T(8,128)(2,1)S(1)} %get-tuple-element.862), channel_id=1, source_target_pairs={{3,0},{0,1},{1,2},{2,3},{7,4},{4,5},{5,6},{6,7},{11,8},{8,9},{9,10... | collective-permute-start | bytes 147464 | tf_op jit(solution)/shard_map/ppermute | solution.py:35
  153.7 5.6 %collective-permute-start.33 = (bf16[16,1536]{1,0:T(8,128)(2,1)S(1)}, bf16[16,1536]{1,0:T(8,128)(2,1)S(1)}, u32[]{:S(2)}, u32[]{:S(2)}) collective-permute-start(bf16[16,1536]{1,0:T(8,128)(2,1)S(1)} %get-tuple-element.864), channel_id=1, source_target_pairs={{2,0},{3,1},{0,2},{1,3},{6,4},{7,5},{4,6},{5,7},{10,8},{11,9},{8,1... | collective-permute-start | bytes 147464 | tf_op jit(solution)/shard_map/ppermute | solution.py:35
  155.8 4.3 %collective-permute-start.34 = (bf16[16,1536]{1,0:T(8,128)(2,1)S(1)}, bf16[16,1536]{1,0:T(8,128)(2,1)S(1)}, u32[]{:S(2)}, u32[]{:S(2)}) collective-permute-start(bf16[16,1536]{1,0:T(8,128)(2,1)S(1)} %get-tuple-element.863), channel_id=1, source_target_pairs={{1,0},{2,1},{3,2},{0,3},{5,4},{6,5},{7,6},{4,7},{9,8},{10,9},{11,1... | collective-permute-start | bytes 147464 | tf_op jit(solution)/shard_map/ppermute | solution.py:35
where the time goes:
time: 162 us; the launch traced here: 161 us
  starting transfers between devices  74.5 us (46%)
  waiting for transfers between devices  41.8 us (26%)
  Pallas kernels  24.2 us (15%)
  local copies, waits for them, and re-layouts  11.9 us (7%)
  other arithmetic  5.8 us (4%)
    ppermute x31, starting transfers between devices, from_peer(): return lax.ppermute(block, axis, [((i + step) % n, i) for i in range(n)])  50.8 us
    ppermute x31, waiting for transfers between devices, from_peer(): return lax.ppermute(block, axis, [((i + step) % n, i) for i in range(n)])  34.1 us
    all_to_all x2, starting transfers between devices, spread(): lax.all_to_all(jnp.broadcast_to(block[None], (peers,) + block.shape), axi...  14.6 us
    pallas_call x2, Pallas kernels, packed_down(): pl.pallas_call(down_kernel, grid_spec=pltpu.PrefetchScalarGridSpec(num_sc...  13.9 us
    pallas_call x2, Pallas kernels, packed_up(): pl.pallas_call(up_kernel, grid_spec=pltpu.PrefetchScalarGridSpec(num_scal...  10.4 us
    all_to_all x2, starting transfers between devices, exchange(): return lax.all_to_all(blocks, axis, split_axis=0, concat_axis=0)  9.12 us
    all_to_all x2, waiting for transfers between devices, spread(): lax.all_to_all(jnp.broadcast_to(block[None], (peers,) + block.shape), axi...  7.68 us
    unnamed x29, local copies, waits for them, and re-layouts  4.61 us
  transfers between devices with their start and end apart: 35, of which 18 were waited for; matrix products, arithmetic and copies ran while one was open for 9% of the time, Pallas kernels for 11%

commit v1 on v0

--- a/solution.py
+++ b/solution.py
@@ -41,28 +41,21 @@
     for k in range(1, n // 2):
         found[k] = from_peer(found[k - 1], axis, 1)
         found[n - k] = from_peer(found[(n + 1 - k) % n], axis, -1)
-    half = block.shape[0] // 2
-    low, high = found[n // 2 - 1], found[n // 2 + 1]
-    low, high, beside = lax.optimization_barrier((low, high, beside))
-    low, high = from_peer(low[:half], axis, 1), from_peer(high[half:], axis, -1)
-    found[n // 2] = jnp.concatenate([low, high])
+    last, beside = lax.optimization_barrier((found[n // 2 - 1], beside))
+    found[n // 2] = from_peer(last, axis, 1)
     return jnp.stack([found[k] for k in range(n)]), beside
 
 
 def ring_total(blocks, axis, beside):
-    n, half = blocks.shape[0], blocks.shape[1] // 2
-    low = from_peer(blocks[n // 2][:half], axis, 1).astype(F32)
-    high = from_peer(blocks[n // 2][half:], axis, -1).astype(F32)
-    down, up = blocks[n // 2 + 1], blocks[n // 2 - 1]
-    down = jnp.concatenate([(down[:half] + low).astype(BF16), down[half:]])
-    up = jnp.concatenate([up[:half], (up[half:] + high).astype(BF16)])
-    for k in range(n // 2 - 2, -1, -1):
-        if k == 0:
-            down, up, beside = lax.optimization_barrier((down, up, beside))
-        down, up = from_peer(down, axis, 1).astype(F32), from_peer(up, axis, -1).astype(F32)
-        if k > 0:
-            down, up = (blocks[n - k] + down).astype(BF16), (blocks[k] + up).astype(BF16)
-    return blocks[0] + down + up, beside
+    n = blocks.shape[0]
+    down, up = blocks[n // 2], blocks[n // 2 - 1]
+    for k in range(n // 2 - 1, 0, -1):
+        down = (blocks[n - k] + from_peer(down, axis, 1).astype(F32)).astype(BF16)
+        if k < n // 2 - 1:
+            up = (blocks[k] + from_peer(up, axis, -1).astype(F32)).astype(BF16)
+    down, up, beside = lax.optimization_barrier((down, up, beside))
+    mine = blocks[0] + from_peer(down, axis, 1).astype(F32) + from_peer(up, axis, -1).astype(F32)
+    return mine, beside
 
 
 def up_kernel(at_ref, x_ref, w_ref, bias_ref, pos_ref, out_ref, acc):
@@ -125,8 +118,7 @@
     @pl.when(pl.program_id(0) == 0)
     def _():
         slot = lax.broadcasted_iota(I32, (SLOTS, PACK * span), 0)
-        @pl.loop(0, BLOCKS)
-        def _(j):
+        for j in range(BLOCKS):
             b = at_ref[j]
             to = pl.ds(pl.multiple_of(b * span, span), span)
             for q in range(pos_ref.shape[0]):
@@ -240,6 +232,13 @@
     pos = pos.reshape(clusters // PACK, PACK, 2 * BLOCKS, span).transpose(0, 2, 1, 3)
     pos = pos.reshape(clusters // PACK, 2 * BLOCKS, PACK * span)
 
+    second, pos = lax.optimization_barrier((second, pos))
+    near = jnp.stack([second] + [from_peer(second, "y", k) for k in range(1, NY)])
+    near, first = lax.optimization_barrier((near, first))
+    x_1 = spread(first, "y").reshape(tokens, width)
+    x_2, x_1 = ring_spread(near, "z", x_1)
+    x_2 = x_2.reshape(tokens, width)
+
     groups = picks.T // clusters
     named = jnp.sum(
         (groups[None] == jnp.arange(NZ * NY, dtype=I32)[:, None, None]).astype(F32), axis=1
@@ -248,13 +247,7 @@
     z, y, part = token // (2 * cut * NY), token // (2 * cut) % NY, token // cut % 2
     block = jnp.where(part == 0, (y * NZ + z) * BLOCKS // (NY * NZ), BLOCKS + z * BLOCKS // NZ)
     belongs = (block[:, None] == jnp.arange(2 * BLOCKS, dtype=I32)[None]).astype(BF16)
-    room = jnp.max(jnp.dot(named, belongs, preferred_element_type=F32))
-
-    near = jnp.stack([second] + [from_peer(second, "y", k) for k in range(1, NY)])
-    near, first = lax.optimization_barrier((near, first))
-    x_1 = spread(first, "y").reshape(tokens, width)
-    x_2, (x_1, room) = ring_spread(near, "z", (x_1, room))
-    x_2 = x_2.reshape(tokens, width)
+    fits = jnp.max(jnp.dot(named, belongs, preferred_element_type=F32)) <= SLOTS
 
     order = [((core + j // NX) % NC) * NX + (xi + j % NX) % NX for j in range(BLOCKS)]
     at = jnp.stack(order).astype(I32)
@@ -288,7 +281,7 @@
         done = done + from_peer(out_2[k], "y", -k).astype(F32)
     out = jnp.concatenate([out_1, done.astype(BF16)], axis=0)
     whole = (activations, picks, up_weight, up_bias, down_weight)
-    return lax.cond(room <= SLOTS, lambda: out, lambda: dense(*whole))
+    return lax.cond(fits, lambda: out, lambda: dense(*whole))
 
 
 def solution(mesh):

time: 162 us -> 149 us (0.920)
  starting transfers between devices: 74.5 us -> 59.4 us
  waiting for transfers between devices: 41.8 us -> 49.8 us
  Pallas kernels: 24.2 us -> 21.2 us
  local copies, waits for them, and re-layouts: 11.9 us -> 9.05 us
    ppermute x31 -> x29, starting transfers between devices: 50.8 us -> 37.3 us  [from_peer(): return lax.ppermute(block, axis, [((i + step) % n, i) for i in range(n)])]
    all_to_all x2, waiting for transfers between devices: 0.01 us -> 10.8 us  [exchange(): return lax.all_to_all(blocks, axis, split_axis=0, concat_axis=0)]
    ppermute x31 -> x29, waiting for transfers between devices: 34.1 us -> 29.4 us  [from_peer(): return lax.ppermute(block, axis, [((i + step) % n, i) for i in range(n)])]
    pallas_call x2, Pallas kernels: 13.9 us -> 10.9 us  [packed_down(): pl.pallas_call(down_kernel, grid_spec=pltpu.PrefetchScalarGridSpec(num_sc...]
    all_to_all x2, waiting for transfers between devices: 7.68 us -> 9.61 us  [spread(): lax.all_to_all(jnp.broadcast_to(block[None], (peers,) + block.shape), axi...]
    slice x4 -> x1, local copies, waits for them, and re-layouts: 2.71 us -> 0.82 us  [ring_total(): down, up = (blocks[n // 2], blocks[n // 2 - 1])]
    convert_element_type x6 -> x5, other arithmetic: 0.25 us -> 2.09 us  [the longest x3 1.07 us: ring_total(): down = (blocks[n - k] + from_peer(down, axis, 1).astype(F32)).astype(BF16)]
    unnamed x29 -> x26, local copies, waits for them, and re-layouts: 4.61 us -> 3.65 us
  transfers between devices with their start and end apart: 35 -> 33, of which waited for: 18 -> 21; matrix products, arithmetic and copies ran while one was open for 9% -> 8% of each run, Pallas kernels for 11% -> 11%
where the time goes in v1:
time: 149 us
  starting transfers between devices  59.4 us (40%)
  waiting for transfers between devices  49.8 us (33%)
  Pallas kernels  21.2 us (14%)
  local copies, waits for them, and re-layouts  9.05 us (6%)
  other arithmetic  6.89 us (5%)
    ppermute x29, starting transfers between devices, from_peer(): return lax.ppermute(block, axis, [((i + step) % n, i) for i in range(n)])  37.3 us
    ppermute x29, waiting for transfers between devices, from_peer(): return lax.ppermute(block, axis, [((i + step) % n, i) for i in range(n)])  29.4 us
    all_to_all x2, starting transfers between devices, spread(): lax.all_to_all(jnp.broadcast_to(block[None], (peers,) + block.shape), axi...  13.4 us
    pallas_call x2, Pallas kernels, packed_down(): pl.pallas_call(down_kernel, grid_spec=pltpu.PrefetchScalarGridSpec(num_sc...  10.9 us
    all_to_all x2, waiting for transfers between devices, exchange(): return lax.all_to_all(blocks, axis, split_axis=0, concat_axis=0)  10.8 us
    pallas_call x2, Pallas kernels, packed_up(): pl.pallas_call(up_kernel, grid_spec=pltpu.PrefetchScalarGridSpec(num_scal...  10.3 us
    all_to_all x2, waiting for transfers between devices, spread(): lax.all_to_all(jnp.broadcast_to(block[None], (peers,) + block.shape), axi...  9.61 us
    all_to_all x2, starting transfers between devices, exchange(): return lax.all_to_all(blocks, axis, split_axis=0, concat_axis=0)  8.79 us
  transfers between devices with their start and end apart: 33, of which 21 were waited for; matrix products, arithmetic and copies ran while one was open for 8% of the time, Pallas kernels for 11%

profile of v1, /device:TPU:8, one launch (start us, length us, event | category | flops | bytes accessed | tf_op | source)
XLA Modules:
  0.0 148.8 jit_solution(7584379280968979965)
XLA Ops:
  0.0 0.9 copy.121
  0.9 0.8 broadcast_in_dim.104
  1.7 8.5 %all-to-all-start = ((bf16[8,16,1536]{2,1,0:T(8,128)(2,1)}), bf16[8,16,1536]{2,1,0:T(8,128)(2,1)S(1)}, u32[]{:S(2)}, u32[]{:S(2)}) async-start(bf16[8,16,1536]{2,1,0:T(8,128)(2,1)} %broadcast_in_dim.104), calls=%async_computation | async-start | bytes 786432 | tf_op jit(solution)/shard_map/all_to_all | solution.py:20
  10.2 1.3 compare_reduce_fusion.1
  14.0 2.6 %collective-permute-start.5 = (bf16[16,1536]{1,0:T(8,128)(2,1)S(1)}, bf16[16,1536]{1,0:T(8,128)(2,1)S(1)}, u32[]{:S(2)}, u32[]{:S(2)}) collective-permute-start(bf16[16,1536]{1,0:T(8,128)(2,1)S(1)} %get-tuple-element.717), channel_id=1, source_target_pairs={{2,0},{3,1},{0,2},{1,3},{6,4},{7,5},{4,6},{5,7},{10,8},{11,9},{8,1... | collective-permute-start | bytes 147464 | tf_op jit(solution)/shard_map/ppermute | solution.py:35
  16.5 1.9 %collective-permute-start.6 = (bf16[16,1536]{1,0:T(8,128)(2,1)S(1)}, bf16[16,1536]{1,0:T(8,128)(2,1)S(1)}, u32[]{:S(2)}, u32[]{:S(2)}) collective-permute-start(bf16[16,1536]{1,0:T(8,128)(2,1)S(1)} %get-tuple-element.717), channel_id=1, source_target_pairs={{3,0},{0,1},{1,2},{2,3},{7,4},{4,5},{5,6},{6,7},{11,8},{8,9},{9,10... | collective-permute-start | bytes 147464 | tf_op jit(solution)/shard_map/ppermute | solution.py:35
  18.5 1.0 collective-permute-done.5
  19.6 1.1 collective-permute-done.6
  20.7 4.2 %all-to-all-done = bf16[8,16,1536]{2,1,0:T(8,128)(2,1)S(1)} async-done(((bf16[8,16,1536]{2,1,0:T(8,128)(2,1)}), bf16[8,16,1536]{2,1,0:T(8,128)(2,1)S(1)}, u32[]{:S(2)}, u32[]{:S(2)}) %all-to-all-start) | async-done | bytes 393248 | tf_op jit(solution)/shard_map/all_to_all | solution.py:20
  24.9 2.1 %collective-permute-start.12 = (bf16[4,16,1536]{2,1,0:T(8,128)(2,1)S(1)}, bf16[4,16,1536]{2,1,0:T(8,128)(2,1)}, u32[]{:S(2)}, u32[]{:S(2)}) collective-permute-start(bf16[4,16,1536]{2,1,0:T(8,128)(2,1)S(1)} %pad_maximum_fusion.2), channel_id=1, source_target_pairs={{28,0},{0,4},{4,8},{8,12},{12,16},{16,20},{20,24},{24,28},{29,1},{... | collective-permute-start | bytes 589832 | tf_op jit(solution)/shard_map/ppermute | solution.py:35
  27.0 1.4 broadcast_in_dim.105
  28.3 4.9 %all-to-all-start.1 = ((bf16[4,8,16,1536]{3,2,1,0:T(8,128)(2,1)}), bf16[4,8,16,1536]{3,2,1,0:T(8,128)(2,1)S(1)}, u32[]{:S(2)}, u32[]{:S(2)}) async-start(bf16[4,8,16,1536]{3,2,1,0:T(8,128)(2,1)} %broadcast_in_dim.105), calls=%async_computation.1 | async-start | bytes 3145728 | tf_op jit(solution)/shard_map/all_to_all | solution.py:20
  33.2 1.4 collective-permute-start.8
  34.7 1.0 bitcast_dynamic-update-slice_fusion.10
  35.7 0.7 collective-permute-start.13
  36.3 3.0 %collective-permute-done.8 = bf16[4,16,1536]{2,1,0:T(8,128)(2,1)S(1)} collective-permute-done((bf16[4,16,1536]{2,1,0:T(8,128)(2,1)}, bf16[4,16,1536]{2,1,0:T(8,128)(2,1)S(1)}, u32[]{:S(2)}, u32[]{:S(2)}) %collective-permute-start.8) | collective-permute-done | bytes 196640 | tf_op jit(solution)/shard_map/ppermute | solution.py:35
  39.4 2.4 %collective-permute-start.9 = (bf16[4,16,1536]{2,1,0:T(8,128)(2,1)S(1)}, bf16[4,16,1536]{2,1,0:T(8,128)(2,1)S(1)}, u32[]{:S(2)}, u32[]{:S(2)}) collective-permute-start(bf16[4,16,1536]{2,1,0:T(8,128)(2,1)S(1)} %collective-permute-done.8), channel_id=1, source_target_pairs={{4,0},{8,4},{12,8},{16,12},{20,16},{24,20},{28,24},{0,28},{5,1},{9... | collective-permute-start | bytes 589832 | tf_op jit(solution)/shard_map/ppermute | solution.py:35
  41.8 1.0 collective-permute-done.13
  42.8 2.2 %collective-permute-done.9 = bf16[4,16,1536]{2,1,0:T(8,128)(2,1)S(1)} collective-permute-done((bf16[4,16,1536]{2,1,0:T(8,128)(2,1)S(1)}, bf16[4,16,1536]{2,1,0:T(8,128)(2,1)S(1)}, u32[]{:S(2)}, u32[]{:S(2)}) %collective-permute-start.9) | collective-permute-done | bytes 196640 | tf_op jit(solution)/shard_map/ppermute | solution.py:35
  45.0 0.7 copy-done.2
  45.7 5.4 %all-to-all-done.1 = bf16[4,8,16,1536]{3,2,1,0:T(8,128)(2,1)S(1)} async-done(((bf16[4,8,16,1536]{3,2,1,0:T(8,128)(2,1)}), bf16[4,8,16,1536]{3,2,1,0:T(8,128)(2,1)S(1)}, u32[]{:S(2)}, u32[]{:S(2)}) %all-to-all-start.1) | async-done | bytes 1572896 | tf_op jit(solution)/shard_map/all_to_all | solution.py:20
  51.2 1.5 %collective-permute-start.11 = (bf16[4,16,1536]{2,1,0:T(8,128)(2,1)}, bf16[4,16,1536]{2,1,0:T(8,128)(2,1)S(1)}, u32[]{:S(2)}, u32[]{:S(2)}) collective-permute-start(bf16[4,16,1536]{2,1,0:T(8,128)(2,1)} %copy-done.2), channel_id=1, source_target_pairs={{4,0},{8,4},{12,8},{16,12},{20,16},{24,20},{28,24},{0,28},{5,1},{9... | collective-permute-start | bytes 589832 | tf_op jit(solution)/shard_map/ppermute | solution.py:35
  52.7 5.9 %shard_map.57 = bf16[8,192,128]{2,1,0:T(8,128)(2,1)S(1)} custom-call(s32[8]{0:T(128)S(1)} %stack.92.at_ref, bf16[512,1536]{1,0:T(8,128)(2,1)S(1)} %bitcast.165, bf16[12,1536,128]{2,1,0:T(8,128)(2,1)} %w_ref.5, f32[3,4,128]{2,1,0:T(4,128)S(1)} %reshape.194.bias_ref, s32[3,16,256]{2,1,0:T(8,128)S(1)} %reshape.192.pos_ref), custom_call_target="tpu_custom_call" | custom-call | flops 4831838208 | bytes 9437184 | tf_op jit(solution)/shard_map/pallas_call | solution.py:92
  59.0 0.9 bitcast_dynamic-update-slice_fusion.6
  59.9 0.9 bitcast_dynamic-update-slice_fusion.4
  60.9 4.4 %shard_map.58 = bf16[8,192,128]{2,1,0:T(8,128)(2,1)S(1)} custom-call(s32[8]{0:T(128)S(1)} %stack.92.at_ref, bf16[512,1536]{1,0:T(8,128)(2,1)S(1)} %bitcast.166, bf16[12,1536,128]{2,1,0:T(8,128)(2,1)S(1)} %bitcast.176, f32[3,4,128]{2,1,0:T(4,128)S(1)} %reshape.194.bias_ref, s32[3,16,256]{2,1,0:T(8,128)S(1)} %reshape.192.pos_ref), custom_call_target="tpu_custom_call" | custom-call | flops 4831838208 | bytes 9437184 | tf_op jit(solution)/shard_map/pallas_call | solution.py:92
  65.3 0.6 collective-permute-start.15
  65.9 1.0 collective-permute-done.15
  67.1 1.6 %collective-permute-start.16 = (bf16[384,128]{1,0:T(8,128)(2,1)S(1)}, bf16[384,128]{1,0:T(8,128)(2,1)S(1)}, u32[]{:S(2)}, u32[]{:S(2)}) collective-permute-start(bf16[384,128]{1,0:T(8,128)(2,1)S(1)} %get-tuple-element.856), channel_id=1, source_target_pairs={{192,0},{0,64},{64,128},{128,192},{193,1},{1,65},{65,129},{129,193... | collective-permute-start | bytes 294920 | tf_op jit(solution)/shard_map/ppermute | solution.py:35
  68.7 2.7 %collective-permute-start.17 = (bf16[384,128]{1,0:T(8,128)(2,1)S(1)}, bf16[384,128]{1,0:T(8,128)(2,1)S(1)}, u32[]{:S(2)}, u32[]{:S(2)}) collective-permute-start(bf16[384,128]{1,0:T(8,128)(2,1)S(1)} %get-tuple-element.858), channel_id=1, source_target_pairs={{128,0},{192,64},{0,128},{64,192},{129,1},{193,65},{1,129},{65,193... | collective-permute-start | bytes 294920 | tf_op jit(solution)/shard_map/ppermute | solution.py:35
  71.4 1.4 collective-permute-start.18
  72.8 0.6 collective-permute-done.16
  73.5 3.1 %collective-permute-done.17 = bf16[384,128]{1,0:T(8,128)(2,1)S(1)} collective-permute-done((bf16[384,128]{1,0:T(8,128)(2,1)S(1)}, bf16[384,128]{1,0:T(8,128)(2,1)S(1)}, u32[]{:S(2)}, u32[]{:S(2)}) %collective-permute-start.17) | collective-permute-done | bytes 98336 | tf_op jit(solution)/shard_map/ppermute | solution.py:35
  76.6 2.4 %collective-permute-start.19 = (bf16[384,128]{1,0:T(8,128)(2,1)S(1)}, bf16[384,128]{1,0:T(8,128)(2,1)S(1)}, u32[]{:S(2)}, u32[]{:S(2)}) collective-permute-start(bf16[384,128]{1,0:T(8,128)(2,1)S(1)} %get-tuple-element.847), channel_id=1, source_target_pairs={{64,0},{128,64},{192,128},{0,192},{65,1},{129,65},{193,129},{1,193... | collective-permute-start | bytes 294920 | tf_op jit(solution)/shard_map/ppermute | solution.py:35
  79.0 1.1 collective-permute-start.20
  80.1 0.7 collective-permute-start.21
  80.9 1.9 %collective-permute-done.19 = bf16[384,128]{1,0:T(8,128)(2,1)S(1)} collective-permute-done((bf16[384,128]{1,0:T(8,128)(2,1)S(1)}, bf16[384,128]{1,0:T(8,128)(2,1)S(1)}, u32[]{:S(2)}, u32[]{:S(2)}) %collective-permute-start.19) | collective-permute-done | bytes 98336 | tf_op jit(solution)/shard_map/ppermute | solution.py:35
  82.8 2.3 %collective-permute-done.20 = bf16[384,128]{1,0:T(8,128)(2,1)S(1)} collective-permute-done((bf16[384,128]{1,0:T(8,128)(2,1)S(1)}, bf16[384,128]{1,0:T(8,128)(2,1)S(1)}, u32[]{:S(2)}, u32[]{:S(2)}) %collective-permute-start.20) | collective-permute-done | bytes 98336 | tf_op jit(solution)/shard_map/ppermute | solution.py:35
  85.2 1.0 collective-permute-done.21
  86.4 1.6 %collective-permute-done.22 = bf16[4,384,128]{2,1,0:T(8,128)(2,1)S(1)} collective-permute-done((bf16[4,384,128]{2,1,0:T(8,128)(2,1)S(1)}, bf16[4,384,128]{2,1,0:T(8,128)(2,1)S(1)}, u32[]{:S(2)}, u32[]{:S(2)}) %collective-permute-start.22) | collective-permute-done | bytes 393248 | tf_op jit(solution)/shard_map/ppermute | solution.py:35
  88.1 5.1 %shard_map.59 = bf16[512,1536]{1,0:T(8,128)(2,1)S(1)} custom-call(s32[8]{0:T(128)S(1)} %stack.92.at_ref, bf16[8,384,128]{2,1,0:T(8,128)(2,1)S(1)} %constant_dynamic-update-slice_fusion.2.packed_ref, s32[3,16,256]{2,1,0:T(8,128)S(1)} %reshape.192.pos_ref, bf16[12,128,1536]{2,1,0:T(8,128)(2,1)S(1)} %bitcast.178), custom_call_target="tpu_custom_call" | custom-call | flops 2415919104 | bytes 7340032 | tf_op jit(solution)/shard_map/pallas_call | solution.py:139
  93.2 0.8 fusion.72
  94.0 0.5 collective-permute-start.26
  94.6 2.7 %collective-permute-start.23 = (bf16[4,16,1536]{2,1,0:T(8,128)(2,1)}, bf16[4,16,1536]{2,1,0:T(8,128)(2,1)}, u32[]{:S(2)}, u32[]{:S(2)}) collective-permute-start(bf16[4,16,1536]{2,1,0:T(8,128)(2,1)} %bitcast.48), channel_id=1, source_target_pairs={{4,0},{8,4},{12,8},{16,12},{20,16},{24,20},{28,24},{0,28},{5,1},{9... | collective-permute-start | bytes 589832 | tf_op jit(solution)/shard_map/ppermute | solution.py:35
  97.3 5.8 %shard_map.60 = bf16[512,1536]{1,0:T(8,128)(2,1)} custom-call(s32[8]{0:T(128)S(1)} %stack.92.at_ref, bf16[8,384,128]{2,1,0:T(8,128)(2,1)S(1)} %constant_dynamic-update-slice_fusion.2.packed_ref, s32[3,16,256]{2,1,0:T(8,128)S(1)} %reshape.192.pos_ref, bf16[12,128,1536]{2,1,0:T(8,128)(2,1)S(1)} %bitcast.178), custom_call_target="tpu_custom_call" | custom-call | flops 2415919104 | bytes 7340032 | tf_op jit(solution)/shard_map/pallas_call | solution.py:139
  103.1 4.9 %all-to-all-start.2 = ((bf16[4,8,16,1536]{3,2,1,0:T(8,128)(2,1)}), bf16[4,8,16,1536]{3,2,1,0:T(8,128)(2,1)S(1)}, u32[]{:S(2)}, u32[]{:S(2)}) async-start(bf16[4,8,16,1536]{3,2,1,0:T(8,128)(2,1)} %bitcast.52), calls=%async_computation.2 | async-start | bytes 3145728 | tf_op jit(solution)/shard_map/all_to_all | solution.py:26
  108.0 1.0 fusion.12
  109.3 1.0 fusion.10
  110.3 2.1 %collective-permute-start.27 = (bf16[4,16,1536]{2,1,0:T(8,128)(2,1)S(1)}, bf16[4,16,1536]{2,1,0:T(8,128)(2,1)S(1)}, u32[]{:S(2)}, u32[]{:S(2)}) collective-permute-start(bf16[4,16,1536]{2,1,0:T(8,128)(2,1)S(1)} %fusion.10), channel_id=1, source_target_pairs={{28,0},{0,4},{4,8},{8,12},{12,16},{16,20},{20,24},{24,28},{29,1},{... | collective-permute-start | bytes 589832 | tf_op jit(solution)/shard_map/ppermute | solution.py:35
  112.4 3.0 %collective-permute-done.24 = bf16[4,16,1536]{2,1,0:T(8,128)(2,1)S(1)} collective-permute-done((bf16[4,16,1536]{2,1,0:T(8,128)(2,1)S(1)}, bf16[4,16,1536]{2,1,0:T(8,128)(2,1)S(1)}, u32[]{:S(2)}, u32[]{:S(2)}) %collective-permute-start.24) | collective-permute-done | bytes 196640 | tf_op jit(solution)/shard_map/ppermute | solution.py:35
  115.5 1.6 %collective-permute-start.25 = (bf16[4,16,1536]{2,1,0:T(8,128)(2,1)S(1)}, bf16[4,16,1536]{2,1,0:T(8,128)(2,1)S(1)}, u32[]{:S(2)}, u32[]{:S(2)}) collective-permute-start(bf16[4,16,1536]{2,1,0:T(8,128)(2,1)S(1)} %fusion.13), channel_id=1, source_target_pairs={{4,0},{8,4},{12,8},{16,12},{20,16},{24,20},{28,24},{0,28},{5,1},{9... | collective-permute-start | bytes 589832 | tf_op jit(solution)/shard_map/ppermute | solution.py:35
  117.0 0.7 collective-permute-done.27
  117.8 3.5 %collective-permute-done.25 = bf16[4,16,1536]{2,1,0:T(8,128)(2,1)S(1)} collective-permute-done((bf16[4,16,1536]{2,1,0:T(8,128)(2,1)S(1)}, bf16[4,16,1536]{2,1,0:T(8,128)(2,1)S(1)}, u32[]{:S(2)}, u32[]{:S(2)}) %collective-permute-start.25) | collective-permute-done | bytes 196640 | tf_op jit(solution)/shard_map/ppermute | solution.py:35
  121.3 6.0 %all-to-all-done.2 = bf16[4,8,16,1536]{3,2,1,0:T(8,128)(2,1)S(1)} async-done(((bf16[4,8,16,1536]{3,2,1,0:T(8,128)(2,1)}), bf16[4,8,16,1536]{3,2,1,0:T(8,128)(2,1)S(1)}, u32[]{:S(2)}, u32[]{:S(2)}) %all-to-all-start.2) | async-done | bytes 1572896 | tf_op jit(solution)/shard_map/all_to_all | solution.py:26
  127.3 1.1 reduce_sum.47
  128.7 1.7 %collective-permute-start.29 = (bf16[4,16,1536]{2,1,0:T(8,128)(2,1)S(1)}, bf16[4,16,1536]{2,1,0:T(8,128)(2,1)S(1)}, u32[]{:S(2)}, u32[]{:S(2)}) collective-permute-start(bf16[4,16,1536]{2,1,0:T(8,128)(2,1)S(1)} %fusion.11), channel_id=1, source_target_pairs={{28,0},{0,4},{4,8},{8,12},{12,16},{16,20},{20,24},{24,28},{29,1},{... | collective-permute-start | bytes 589832 | tf_op jit(solution)/shard_map/ppermute | solution.py:35
  130.4 0.9 convert_reduce_fusion
  131.3 3.9 %all-to-all-start.3 = ((bf16[8,16,1536]{2,1,0:T(8,128)(2,1)}), bf16[8,16,1536]{2,1,0:T(8,128)(2,1)S(1)}, u32[]{:S(2)}, u32[]{:S(2)}) async-start(bf16[8,16,1536]{2,1,0:T(8,128)(2,1)} %reduce_sum.47), calls=%async_computation.3 | async-start | bytes 786432 | tf_op jit(solution)/shard_map/all_to_all | solution.py:26
  135.7 3.5 %collective-permute-start.31 = (bf16[16,1536]{1,0:T(8,128)(2,1)S(1)}, bf16[16,1536]{1,0:T(8,128)(2,1)S(1)}, u32[]{:S(2)}, u32[]{:S(2)}) collective-permute-start(bf16[16,1536]{1,0:T(8,128)(2,1)S(1)} %get-tuple-element.861), channel_id=1, source_target_pairs={{2,0},{3,1},{0,2},{1,3},{6,4},{7,5},{4,6},{5,7},{10,8},{11,9},{8,1... | collective-permute-start | bytes 147464 | tf_op jit(solution)/shard_map/ppermute | solution.py:35
  139.3 0.6 collective-permute-start.32
  139.8 1.0 convolution_reduce_fusion
  141.5 1.8 %collective-permute-done.32 = bf16[16,1536]{1,0:T(8,128)(2,1)S(1)} collective-permute-done((bf16[16,1536]{1,0:T(8,128)(2,1)S(1)}, bf16[16,1536]{1,0:T(8,128)(2,1)S(1)}, u32[]{:S(2)}, u32[]{:S(2)}) %collective-permute-start.32) | collective-permute-done | bytes 49184 | tf_op jit(solution)/shard_map/ppermute | solution.py:35
  143.4 4.8 %all-to-all-done.3 = bf16[8,16,1536]{2,1,0:T(8,128)(2,1)S(1)} async-done(((bf16[8,16,1536]{2,1,0:T(8,128)(2,1)}), bf16[8,16,1536]{2,1,0:T(8,128)(2,1)S(1)}, u32[]{:S(2)}, u32[]{:S(2)}) %all-to-all-start.3) | async-done | bytes 393248 | tf_op jit(solution)/shard_map/all_to_all | solution.py:26
  148.2 0.6 pad_maximum_fusion.3
  (85 shorter events, 4.9 us)
Async XLA Ops:
  0.0 18.4 %copy-start.3 = (f32[12,128]{1,0:T(8,128)S(1)}, f32[12,128]{1,0:T(8,128)}, u32[]{:S(2)}) copy-start(f32[12,128]{1,0:T(8,128)} %param.20) | copy-start | bytes 18436
  1.7 23.2 %all-to-all-start = ((bf16[8,16,1536]{2,1,0:T(8,128)(2,1)}), bf16[8,16,1536]{2,1,0:T(8,128)(2,1)S(1)}, u32[]{:S(2)}, u32[]{:S(2)}) async-start(bf16[8,16,1536]{2,1,0:T(8,128)(2,1)} %broadcast_in_dim.104), calls=%async_computation | async-start | bytes 786432 | tf_op jit(solution)/shard_map/all_to_all | solution.py:20
  13.4 5.1 %collective-permute-start.4 = (bf16[16,1536]{1,0:T(8,128)(2,1)S(1)}, bf16[16,1536]{1,0:T(8,128)(2,1)S(1)}, u32[]{:S(2)}, u32[]{:S(2)}) collective-permute-start(bf16[16,1536]{1,0:T(8,128)(2,1)S(1)} %get-tuple-element.717), channel_id=1, source_target_pairs={{1,0},{2,1},{3,2},{0,3},{5,4},{6,5},{7,6},{4,7},{9,8},{10,9},{11,1... | collective-permute-start | bytes 147464 | tf_op jit(solution)/shard_map/ppermute | solution.py:35
  14.0 5.6 %collective-permute-start.5 = (bf16[16,1536]{1,0:T(8,128)(2,1)S(1)}, bf16[16,1536]{1,0:T(8,128)(2,1)S(1)}, u32[]{:S(2)}, u32[]{:S(2)}) collective-permute-start(bf16[16,1536]{1,0:T(8,128)(2,1)S(1)} %get-tuple-element.717), channel_id=1, source_target_pairs={{2,0},{3,1},{0,2},{1,3},{6,4},{7,5},{4,6},{5,7},{10,8},{11,9},{8,1... | collective-permute-start | bytes 147464 | tf_op jit(solution)/shard_map/ppermute | solution.py:35
  16.5 4.1 %collective-permute-start.6 = (bf16[16,1536]{1,0:T(8,128)(2,1)S(1)}, bf16[16,1536]{1,0:T(8,128)(2,1)S(1)}, u32[]{:S(2)}, u32[]{:S(2)}) collective-permute-start(bf16[16,1536]{1,0:T(8,128)(2,1)S(1)} %get-tuple-element.717), channel_id=1, source_target_pairs={{3,0},{0,1},{1,2},{2,3},{7,4},{4,5},{5,6},{6,7},{11,8},{8,9},{9,10... | collective-permute-start | bytes 147464 | tf_op jit(solution)/shard_map/ppermute | solution.py:35
  24.8 8.4 %collective-permute-start.7 = (bf16[4,16,1536]{2,1,0:T(8,128)(2,1)S(1)}, bf16[4,16,1536]{2,1,0:T(8,128)(2,1)}, u32[]{:S(2)}, u32[]{:S(2)}) collective-permute-start(bf16[4,16,1536]{2,1,0:T(8,128)(2,1)S(1)} %pad_maximum_fusion.2), channel_id=1, source_target_pairs={{4,0},{8,4},{12,8},{16,12},{20,16},{24,20},{28,24},{0,28},{5,1},{9... | collective-permute-start | bytes 589832 | tf_op jit(solution)/shard_map/ppermute | solution.py:35
  24.9 10.8 %collective-permute-start.12 = (bf16[4,16,1536]{2,1,0:T(8,128)(2,1)S(1)}, bf16[4,16,1536]{2,1,0:T(8,128)(2,1)}, u32[]{:S(2)}, u32[]{:S(2)}) collective-permute-start(bf16[4,16,1536]{2,1,0:T(8,128)(2,1)S(1)} %pad_maximum_fusion.2), channel_id=1, source_target_pairs={{28,0},{0,4},{4,8},{8,12},{12,16},{16,20},{20,24},{24,28},{29,1},{... | collective-permute-start | bytes 589832 | tf_op jit(solution)/shard_map/ppermute | solution.py:35
  28.3 22.8 %all-to-all-start.1 = ((bf16[4,8,16,1536]{3,2,1,0:T(8,128)(2,1)}), bf16[4,8,16,1536]{3,2,1,0:T(8,128)(2,1)S(1)}, u32[]{:S(2)}, u32[]{:S(2)}) async-start(bf16[4,8,16,1536]{3,2,1,0:T(8,128)(2,1)} %broadcast_in_dim.105), calls=%async_computation.1 | async-start | bytes 3145728 | tf_op jit(solution)/shard_map/all_to_all | solution.py:20
  33.2 6.1 %collective-permute-start.8 = (bf16[4,16,1536]{2,1,0:T(8,128)(2,1)}, bf16[4,16,1536]{2,1,0:T(8,128)(2,1)S(1)}, u32[]{:S(2)}, u32[]{:S(2)}) collective-permute-start(bf16[4,16,1536]{2,1,0:T(8,128)(2,1)} %collective-permute-done.7), channel_id=1, source_target_pairs={{4,0},{8,4},{12,8},{16,12},{20,16},{24,20},{28,24},{0,28},{5,1},{9... | collective-permute-start | bytes 589832 | tf_op jit(solution)/shard_map/ppermute | solution.py:35
  35.7 7.2 %collective-permute-start.13 = (bf16[4,16,1536]{2,1,0:T(8,128)(2,1)}, bf16[4,16,1536]{2,1,0:T(8,128)(2,1)S(1)}, u32[]{:S(2)}, u32[]{:S(2)}) collective-permute-start(bf16[4,16,1536]{2,1,0:T(8,128)(2,1)} %collective-permute-done.12), channel_id=1, source_target_pairs={{28,0},{0,4},{4,8},{8,12},{12,16},{16,20},{20,24},{24,28},{29,1},{... | collective-permute-start | bytes 589832 | tf_op jit(solution)/shard_map/ppermute | solution.py:35
  39.4 5.7 %collective-permute-start.9 = (bf16[4,16,1536]{2,1,0:T(8,128)(2,1)S(1)}, bf16[4,16,1536]{2,1,0:T(8,128)(2,1)S(1)}, u32[]{:S(2)}, u32[]{:S(2)}) collective-permute-start(bf16[4,16,1536]{2,1,0:T(8,128)(2,1)S(1)} %collective-permute-done.8), channel_id=1, source_target_pairs={{4,0},{8,4},{12,8},{16,12},{20,16},{24,20},{28,24},{0,28},{5,1},{9... | collective-permute-start | bytes 589832 | tf_op jit(solution)/shard_map/ppermute | solution.py:35
  42.8 16.1 %collective-permute-start.14 = (bf16[4,16,1536]{2,1,0:T(8,128)(2,1)S(1)}, bf16[4,16,1536]{2,1,0:T(8,128)(2,1)}, u32[]{:S(2)}, u32[]{:S(2)}) collective-permute-start(bf16[4,16,1536]{2,1,0:T(8,128)(2,1)S(1)} %collective-permute-done.13), channel_id=1, source_target_pairs={{28,0},{0,4},{4,8},{8,12},{12,16},{16,20},{20,24},{24,28},{29,1},{... | collective-permute-start | bytes 589832 | tf_op jit(solution)/shard_map/ppermute | solution.py:35
  45.0 0.7 copy-start.2
  51.2 9.7 %slice-start = ((s8[4718592]{0:T(1024)(128)(4,1)}), s8[4194304]{0:T(1024)(128)(4,1)S(1)}, s32[]{:S(2)}) async-start(s8[4718592]{0:T(1024)(128)(4,1)} %bitcast.175), calls=%async_computation.4 | async-start | bytes 8388608
  51.2 9.7 %slice-start.1 = ((s8[4718592]{0:T(1024)(128)(4,1)}), s8[524288]{0:T(1024)(128)(4,1)S(1)}, s32[]{:S(2)}) async-start(s8[4718592]{0:T(1024)(128)(4,1)} %bitcast.175), calls=%async_computation.5 | async-start | bytes 1048576
  51.2 7.7 %collective-permute-start.11 = (bf16[4,16,1536]{2,1,0:T(8,128)(2,1)}, bf16[4,16,1536]{2,1,0:T(8,128)(2,1)S(1)}, u32[]{:S(2)}, u32[]{:S(2)}) collective-permute-start(bf16[4,16,1536]{2,1,0:T(8,128)(2,1)} %copy-done.2), channel_id=1, source_target_pairs={{4,0},{8,4},{12,8},{16,12},{20,16},{24,20},{28,24},{0,28},{5,1},{9... | collective-permute-start | bytes 589832 | tf_op jit(solution)/shard_map/ppermute | solution.py:35
  58.6 7.3 %collective-permute-start.10 = (bf16[4,192,128]{2,1,0:T(8,128)(2,1)S(1)}, bf16[4,192,128]{2,1,0:T(8,128)(2,1)S(1)}, u32[]{:S(2)}, u32[]{:S(2)}) collective-permute-start(bf16[4,192,128]{2,1,0:T(8,128)(2,1)S(1)} %slice.107), channel_id=1, source_target_pairs={{32,0},{0,32},{33,1},{1,33},{34,2},{2,34},{35,3},{3,35},{36,4},{4,... | collective-permute-start | bytes 589832 | tf_op jit(solution)/shard_map/ppermute | solution.py:35
  60.9 27.2 %slice-start.2 = ((s8[4718592]{0:T(1024)(128)(4,1)}), s8[4194304]{0:T(1024)(128)(4,1)S(1)}, s32[]{:S(2)}) async-start(s8[4718592]{0:T(1024)(128)(4,1)} %bitcast.177), calls=%async_computation.6 | async-start | bytes 8388608
  60.9 27.2 %slice-start.3 = ((s8[4718592]{0:T(1024)(128)(4,1)}), s8[524288]{0:T(1024)(128)(4,1)S(1)}, s32[]{:S(2)}) async-start(s8[4718592]{0:T(1024)(128)(4,1)} %bitcast.177), calls=%async_computation.7 | async-start | bytes 1048576
  65.3 15.5 %copy-start.1 = (s32[1024,48]{0,1:T(8,128)S(1)}, s32[1024,48]{0,1:T(8,128)}, u32[]{:S(2)}) copy-start(s32[1024,48]{0,1:T(8,128)} %param.18) | copy-start | bytes 589828
  65.3 1.6 %collective-permute-start.15 = (bf16[4,192,128]{2,1,0:T(8,128)(2,1)S(1)}, bf16[4,192,128]{2,1,0:T(8,128)(2,1)S(1)}, u32[]{:S(2)}, u32[]{:S(2)}) collective-permute-start(bf16[4,192,128]{2,1,0:T(8,128)(2,1)S(1)} %slice.109), channel_id=1, source_target_pairs={{32,0},{0,32},{33,1},{1,33},{34,2},{2,34},{35,3},{3,35},{36,4},{4,... | collective-permute-start | bytes 589832 | tf_op jit(solution)/shard_map/ppermute | solution.py:35
  67.1 6.4 %collective-permute-start.16 = (bf16[384,128]{1,0:T(8,128)(2,1)S(1)}, bf16[384,128]{1,0:T(8,128)(2,1)S(1)}, u32[]{:S(2)}, u32[]{:S(2)}) collective-permute-start(bf16[384,128]{1,0:T(8,128)(2,1)S(1)} %get-tuple-element.856), channel_id=1, source_target_pairs={{192,0},{0,64},{64,128},{128,192},{193,1},{1,65},{65,129},{129,193... | collective-permute-start | bytes 294920 | tf_op jit(solution)/shard_map/ppermute | solution.py:35
  68.7 7.9 %collective-permute-start.17 = (bf16[384,128]{1,0:T(8,128)(2,1)S(1)}, bf16[384,128]{1,0:T(8,128)(2,1)S(1)}, u32[]{:S(2)}, u32[]{:S(2)}) collective-permute-start(bf16[384,128]{1,0:T(8,128)(2,1)S(1)} %get-tuple-element.858), channel_id=1, source_target_pairs={{128,0},{192,64},{0,128},{64,192},{129,1},{193,65},{1,129},{65,193... | collective-permute-start | bytes 294920 | tf_op jit(solution)/shard_map/ppermute | solution.py:35
  71.4 5.1 %collective-permute-start.18 = (bf16[384,128]{1,0:T(8,128)(2,1)S(1)}, bf16[384,128]{1,0:T(8,128)(2,1)S(1)}, u32[]{:S(2)}, u32[]{:S(2)}) collective-permute-start(bf16[384,128]{1,0:T(8,128)(2,1)S(1)} %get-tuple-element.857), channel_id=1, source_target_pairs={{64,0},{128,64},{192,128},{0,192},{65,1},{129,65},{193,129},{1,193... | collective-permute-start | bytes 294920 | tf_op jit(solution)/shard_map/ppermute | solution.py:35
  76.6 6.2 %collective-permute-start.19 = (bf16[384,128]{1,0:T(8,128)(2,1)S(1)}, bf16[384,128]{1,0:T(8,128)(2,1)S(1)}, u32[]{:S(2)}, u32[]{:S(2)}) collective-permute-start(bf16[384,128]{1,0:T(8,128)(2,1)S(1)} %get-tuple-element.847), channel_id=1, source_target_pairs={{64,0},{128,64},{192,128},{0,192},{65,1},{129,65},{193,129},{1,193... | collective-permute-start | bytes 294920 | tf_op jit(solution)/shard_map/ppermute | solution.py:35
  79.0 6.2 %collective-permute-start.20 = (bf16[384,128]{1,0:T(8,128)(2,1)S(1)}, bf16[384,128]{1,0:T(8,128)(2,1)S(1)}, u32[]{:S(2)}, u32[]{:S(2)}) collective-permute-start(bf16[384,128]{1,0:T(8,128)(2,1)S(1)} %get-tuple-element.847), channel_id=1, source_target_pairs={{128,0},{192,64},{0,128},{64,192},{129,1},{193,65},{1,129},{65,193... | collective-permute-start | bytes 294920 | tf_op jit(solution)/shard_map/ppermute | solution.py:35
  80.1 6.1 %collective-permute-start.21 = (bf16[384,128]{1,0:T(8,128)(2,1)S(1)}, bf16[384,128]{1,0:T(8,128)(2,1)S(1)}, u32[]{:S(2)}, u32[]{:S(2)}) collective-permute-start(bf16[384,128]{1,0:T(8,128)(2,1)S(1)} %get-tuple-element.847), channel_id=1, source_target_pairs={{192,0},{0,64},{64,128},{128,192},{193,1},{1,65},{65,129},{129,193... | collective-permute-start | bytes 294920 | tf_op jit(solution)/shard_map/ppermute | solution.py:35
  86.2 1.8 %collective-permute-start.22 = (bf16[4,384,128]{2,1,0:T(8,128)(2,1)S(1)}, bf16[4,384,128]{2,1,0:T(8,128)(2,1)S(1)}, u32[]{:S(2)}, u32[]{:S(2)}) collective-permute-start(bf16[4,384,128]{2,1,0:T(8,128)(2,1)S(1)} %pad_maximum_fusion.1), channel_id=1, source_target_pairs={{32,0},{0,32},{33,1},{1,33},{34,2},{2,34},{35,3},{3,35},{36,4},{4,... | collective-permute-start | bytes 1179656 | tf_op jit(solution)/shard_map/ppermute | solution.py:35
  94.0 15.3 %collective-permute-start.26 = (bf16[4,16,1536]{2,1,0:T(8,128)(2,1)S(1)}, bf16[4,16,1536]{2,1,0:T(8,128)(2,1)}, u32[]{:S(2)}, u32[]{:S(2)}) collective-permute-start(bf16[4,16,1536]{2,1,0:T(8,128)(2,1)S(1)} %bitcast.190), channel_id=1, source_target_pairs={{28,0},{0,4},{4,8},{8,12},{12,16},{16,20},{20,24},{24,28},{29,1},{... | collective-permute-start | bytes 589832 | tf_op jit(solution)/shard_map/ppermute | solution.py:35
  94.6 13.5 %collective-permute-start.23 = (bf16[4,16,1536]{2,1,0:T(8,128)(2,1)}, bf16[4,16,1536]{2,1,0:T(8,128)(2,1)}, u32[]{:S(2)}, u32[]{:S(2)}) collective-permute-start(bf16[4,16,1536]{2,1,0:T(8,128)(2,1)} %bitcast.48), channel_id=1, source_target_pairs={{4,0},{8,4},{12,8},{16,12},{20,16},{24,20},{28,24},{0,28},{5,1},{9... | collective-permute-start | bytes 589832 | tf_op jit(solution)/shard_map/ppermute | solution.py:35
  103.1 24.2 %all-to-all-start.2 = ((bf16[4,8,16,1536]{3,2,1,0:T(8,128)(2,1)}), bf16[4,8,16,1536]{3,2,1,0:T(8,128)(2,1)S(1)}, u32[]{:S(2)}, u32[]{:S(2)}) async-start(bf16[4,8,16,1536]{3,2,1,0:T(8,128)(2,1)} %bitcast.52), calls=%async_computation.2 | async-start | bytes 3145728 | tf_op jit(solution)/shard_map/all_to_all | solution.py:26
  109.0 6.4 %collective-permute-start.24 = (bf16[4,16,1536]{2,1,0:T(8,128)(2,1)S(1)}, bf16[4,16,1536]{2,1,0:T(8,128)(2,1)S(1)}, u32[]{:S(2)}, u32[]{:S(2)}) collective-permute-start(bf16[4,16,1536]{2,1,0:T(8,128)(2,1)S(1)} %fusion.12), channel_id=1, source_target_pairs={{4,0},{8,4},{12,8},{16,12},{20,16},{24,20},{28,24},{0,28},{5,1},{9... | collective-permute-start | bytes 589832 | tf_op jit(solution)/shard_map/ppermute | solution.py:35
  110.3 7.4 %collective-permute-start.27 = (bf16[4,16,1536]{2,1,0:T(8,128)(2,1)S(1)}, bf16[4,16,1536]{2,1,0:T(8,128)(2,1)S(1)}, u32[]{:S(2)}, u32[]{:S(2)}) collective-permute-start(bf16[4,16,1536]{2,1,0:T(8,128)(2,1)S(1)} %fusion.10), channel_id=1, source_target_pairs={{28,0},{0,4},{4,8},{8,12},{12,16},{16,20},{20,24},{24,28},{29,1},{... | collective-permute-start | bytes 589832 | tf_op jit(solution)/shard_map/ppermute | solution.py:35
  115.5 5.7 %collective-permute-start.25 = (bf16[4,16,1536]{2,1,0:T(8,128)(2,1)S(1)}, bf16[4,16,1536]{2,1,0:T(8,128)(2,1)S(1)}, u32[]{:S(2)}, u32[]{:S(2)}) collective-permute-start(bf16[4,16,1536]{2,1,0:T(8,128)(2,1)S(1)} %fusion.13), channel_id=1, source_target_pairs={{4,0},{8,4},{12,8},{16,12},{20,16},{24,20},{28,24},{0,28},{5,1},{9... | collective-permute-start | bytes 589832 | tf_op jit(solution)/shard_map/ppermute | solution.py:35
  128.4 6.8 %collective-permute-start.28 = (bf16[4,16,1536]{2,1,0:T(8,128)(2,1)S(1)}, bf16[4,16,1536]{2,1,0:T(8,128)(2,1)S(1)}, u32[]{:S(2)}, u32[]{:S(2)}) collective-permute-start(bf16[4,16,1536]{2,1,0:T(8,128)(2,1)S(1)} %fusion.14), channel_id=1, source_target_pairs={{4,0},{8,4},{12,8},{16,12},{20,16},{24,20},{28,24},{0,28},{5,1},{9... | collective-permute-start | bytes 589832 | tf_op jit(solution)/shard_map/ppermute | solution.py:35
  128.7 6.9 %collective-permute-start.29 = (bf16[4,16,1536]{2,1,0:T(8,128)(2,1)S(1)}, bf16[4,16,1536]{2,1,0:T(8,128)(2,1)S(1)}, u32[]{:S(2)}, u32[]{:S(2)}) collective-permute-start(bf16[4,16,1536]{2,1,0:T(8,128)(2,1)S(1)} %fusion.11), channel_id=1, source_target_pairs={{28,0},{0,4},{4,8},{8,12},{12,16},{16,20},{20,24},{24,28},{29,1},{... | collective-permute-start | bytes 589832 | tf_op jit(solution)/shard_map/ppermute | solution.py:35
  131.3 16.8 %all-to-all-start.3 = ((bf16[8,16,1536]{2,1,0:T(8,128)(2,1)}), bf16[8,16,1536]{2,1,0:T(8,128)(2,1)S(1)}, u32[]{:S(2)}, u32[]{:S(2)}) async-start(bf16[8,16,1536]{2,1,0:T(8,128)(2,1)} %reduce_sum.47), calls=%async_computation.3 | async-start | bytes 786432 | tf_op jit(solution)/shard_map/all_to_all | solution.py:26
  135.7 5.9 %collective-permute-start.30 = (bf16[16,1536]{1,0:T(8,128)(2,1)S(1)}, bf16[16,1536]{1,0:T(8,128)(2,1)S(1)}, u32[]{:S(2)}, u32[]{:S(2)}) collective-permute-start(bf16[16,1536]{1,0:T(8,128)(2,1)S(1)} %get-tuple-element.859), channel_id=1, source_target_pairs={{3,0},{0,1},{1,2},{2,3},{7,4},{4,5},{5,6},{6,7},{11,8},{8,9},{9,10... | collective-permute-start | bytes 147464 | tf_op jit(solution)/shard_map/ppermute | solution.py:35
  135.7 5.8 %collective-permute-start.31 = (bf16[16,1536]{1,0:T(8,128)(2,1)S(1)}, bf16[16,1536]{1,0:T(8,128)(2,1)S(1)}, u32[]{:S(2)}, u32[]{:S(2)}) collective-permute-start(bf16[16,1536]{1,0:T(8,128)(2,1)S(1)} %get-tuple-element.861), channel_id=1, source_target_pairs={{2,0},{3,1},{0,2},{1,3},{6,4},{7,5},{4,6},{5,7},{10,8},{11,9},{8,1... | collective-permute-start | bytes 147464 | tf_op jit(solution)/shard_map/ppermute | solution.py:35
  139.3 4.1 %collective-permute-start.32 = (bf16[16,1536]{1,0:T(8,128)(2,1)S(1)}, bf16[16,1536]{1,0:T(8,128)(2,1)S(1)}, u32[]{:S(2)}, u32[]{:S(2)}) collective-permute-start(bf16[16,1536]{1,0:T(8,128)(2,1)S(1)} %get-tuple-element.860), channel_id=1, source_target_pairs={{1,0},{2,1},{3,2},{0,3},{5,4},{6,5},{7,6},{4,7},{9,8},{10,9},{11,1... | collective-permute-start | bytes 147464 | tf_op jit(solution)/shard_map/ppermute | solution.py:35

commit v2 on v1

--- a/solution.py
+++ b/solution.py
@@ -43,28 +43,30 @@
         found[n - k] = from_peer(found[(n + 1 - k) % n], axis, -1)
     last, beside = lax.optimization_barrier((found[n // 2 - 1], beside))
     found[n // 2] = from_peer(last, axis, 1)
-    return jnp.stack([found[k] for k in range(n)]), beside
-
-
-def ring_total(blocks, axis, beside):
+    return [found[k] for k in range(n)], beside
+
+
+def ring_total(blocks, axis):
     n = blocks.shape[0]
     down, up = blocks[n // 2], blocks[n // 2 - 1]
     for k in range(n // 2 - 1, 0, -1):
         down = (blocks[n - k] + from_peer(down, axis, 1).astype(F32)).astype(BF16)
         if k < n // 2 - 1:
             up = (blocks[k] + from_peer(up, axis, -1).astype(F32)).astype(BF16)
-    down, up, beside = lax.optimization_barrier((down, up, beside))
-    mine = blocks[0] + from_peer(down, axis, 1).astype(F32) + from_peer(up, axis, -1).astype(F32)
-    return mine, beside
-
-
-def up_kernel(at_ref, x_ref, w_ref, bias_ref, pos_ref, out_ref, acc):
+    return blocks[0] + from_peer(down, axis, 1).astype(F32) + from_peer(up, axis, -1).astype(F32)
+
+
+def up_kernel(at_ref, *refs):
+    *pieces, w_ref, bias_ref, pos_ref, out_ref, acc, x_ref = refs
     span, neurons = x_ref.shape[0] // BLOCKS, w_ref.shape[-1]
     slot = lax.broadcasted_iota(I32, (SLOTS, PACK * span), 0)
 
     @pl.when(pl.program_id(0) == 0)
     def _():
         acc[...] = jnp.zeros_like(acc)
+        rows = x_ref.shape[0] // len(pieces)
+        for k, piece in enumerate(pieces):
+            x_ref[k * rows : (k + 1) * rows] = piece[...]
 
     pairs = []
     for p in range(0, PACK, 2):
@@ -86,29 +88,33 @@
             out_ref[j] = acc[at_ref[j]].astype(BF16)
 
 
-def packed_up(at, x, up_weight, bias, pos, part):
+def packed_up(at, pieces, up_weight, bias, pos, part):
     clusters, width, neurons = up_weight.shape
-    tokens = x.shape[0]
+    rows = pieces[0].shape[0]
+    tokens = rows * len(pieces)
     return pl.pallas_call(
         up_kernel,
         grid_spec=pltpu.PrefetchScalarGridSpec(
             num_scalar_prefetch=1,
             grid=(clusters // PACK,),
             in_specs=[
-                pl.BlockSpec((tokens, width), lambda i, at: (0, 0)),
+                *[pl.BlockSpec((rows, width), lambda i, at: (0, 0)) for _ in pieces],
                 pl.BlockSpec((PACK, width, neurons), lambda i, at: (i, 0, 0)),
                 pl.BlockSpec((1, PACK, neurons), lambda i, at: (i, 0, 0)),
                 pl.BlockSpec((1, BLOCKS, PACK * tokens // BLOCKS), lambda i, at: (i, part, 0)),
             ],
             out_specs=pl.BlockSpec((BLOCKS, SLOTS, neurons), lambda i, at: (0, 0, 0)),
-            scratch_shapes=[pltpu.VMEM((BLOCKS, SLOTS, neurons), F32)],
+            scratch_shapes=[
+                pltpu.VMEM((BLOCKS, SLOTS, neurons), F32),
+                pltpu.VMEM((tokens, width), BF16),
+            ],
         ),
         out_shape=jax.ShapeDtypeStruct((BLOCKS, SLOTS, neurons), BF16),
         compiler_params=pltpu.CompilerParams(vmem_limit_bytes=VMEM),
         cost_estimate=pl.CostEstimate(
             flops=4 * tokens * width * clusters * neurons, bytes_accessed=9 << 20, transcendentals=0
         ),
-    )(at, x, up_weight, bias, pos)
+    )(at, *pieces, up_weight, bias, pos)
 
 
 def down_kernel(at_ref, packed_ref, pos_ref, w_ref, out_ref, hidden):
@@ -237,7 +243,7 @@
     near, first = lax.optimization_barrier((near, first))
     x_1 = spread(first, "y").reshape(tokens, width)
     x_2, x_1 = ring_spread(near, "z", x_1)
-    x_2 = x_2.reshape(tokens, width)
+    x_2 = [x.reshape(tokens // NZ, width) for x in x_2]
 
     groups = picks.T // clusters
     named = jnp.sum(
@@ -268,14 +274,13 @@
         own = jnp.stack([own] + [from_peer(own, "x", k) for k in range(1, NX)])
         return jnp.concatenate([own, from_peer(own, "core", 1)], axis=0)
 
-    rows_1, rows_2 = pair_of(x_1, 0), pair_of(x_2, 1)
+    rows_1, rows_2 = pair_of([x_1], 0), pair_of(x_2, 1)
     packed = all_of(sum_of(jnp.concatenate([rows_1, rows_2], axis=1)))
     out_1 = packed_down(at, packed, pos, down_weight, tokens, 0).reshape(NY, NZ, cut, width)
     out_2 = packed_down(at, packed, pos, down_weight, tokens, 1).reshape(NZ, NY, cut, width)
     out_1 = total(exchange(out_1, "y")).astype(BF16)
-    out_2, out_1 = ring_total(out_2, "z", out_1)
+    out_2 = ring_total(out_2, "z").astype(BF16)
     out_1 = total(exchange(out_1, "z")).astype(BF16)
-    out_2 = out_2.astype(BF16)
     done = out_2[0].astype(F32)
     for k in range(1, NY):
         done = done + from_peer(out_2[k], "y", -k).astype(F32)

time: 149 us -> 147 us (0.987)
  starting transfers between devices: 59.4 us -> 66.6 us
  waiting for transfers between devices: 49.8 us -> 43.2 us
  local copies, waits for them, and re-layouts: 9.05 us -> 5.59 us
    all_to_all x2, waiting for transfers between devices: 10.8 us -> 4.71 us  [exchange(): return lax.all_to_all(blocks, axis, split_axis=0, concat_axis=0)]
    all_to_all x2, waiting for transfers between devices: 9.61 us -> 4.74 us  [spread(): lax.all_to_all(jnp.broadcast_to(block[None], (peers,) + block.shape), axi...]
    ppermute x29, waiting for transfers between devices: 29.4 us -> 33.7 us  [from_peer(): return lax.ppermute(block, axis, [((i + step) % n, i) for i in range(n)])]
    ppermute x29, starting transfers between devices: 37.3 us -> 41.4 us  [from_peer(): return lax.ppermute(block, axis, [((i + step) % n, i) for i in range(n)])]
    all_to_all x2, starting transfers between devices: 8.79 us -> 11.8 us  [exchange(): return lax.all_to_all(blocks, axis, split_axis=0, concat_axis=0)]
    unnamed x26 -> x23, local copies, waits for them, and re-layouts: 3.65 us -> 0.99 us
  transfers between devices with their start and end apart: 33 -> 33, of which waited for: 21 -> 20; matrix products, arithmetic and copies ran while one was open for 8% -> 5% of each run, Pallas kernels for 11% -> 11%
where the time goes in v2:
time: 147 us; the launch traced here: 146 us
  starting transfers between devices  66.6 us (45%)
  waiting for transfers between devices  43.2 us (29%)
  Pallas kernels  21.4 us (15%)
  other arithmetic  6.89 us (5%)
  local copies, waits for them, and re-layouts  5.59 us (4%)
    ppermute x29, starting transfers between devices, from_peer(): return lax.ppermute(block, axis, [((i + step) % n, i) for i in range(n)])  41.4 us
    ppermute x29, waiting for transfers between devices, from_peer(): return lax.ppermute(block, axis, [((i + step) % n, i) for i in range(n)])  33.7 us
    all_to_all x2, starting transfers between devices, spread(): lax.all_to_all(jnp.broadcast_to(block[None], (peers,) + block.shape), axi...  13.4 us
    all_to_all x2, starting transfers between devices, exchange(): return lax.all_to_all(blocks, axis, split_axis=0, concat_axis=0)  11.8 us
    pallas_call x2, Pallas kernels, packed_down(): pl.pallas_call(down_kernel, grid_spec=pltpu.PrefetchScalarGridSpec(num_sc...  10.9 us
    pallas_call x2, Pallas kernels, packed_up(): pl.pallas_call(up_kernel, grid_spec=pltpu.PrefetchScalarGridSpec(num_scal...  10.5 us
    all_to_all x2, waiting for transfers between devices, spread(): lax.all_to_all(jnp.broadcast_to(block[None], (peers,) + block.shape), axi...  4.74 us
    all_to_all x2, waiting for transfers between devices, exchange(): return lax.all_to_all(blocks, axis, split_axis=0, concat_axis=0)  4.71 us
  transfers between devices with their start and end apart: 33, of which 20 were waited for; matrix products, arithmetic and copies ran while one was open for 5% of the time, Pallas kernels for 11%

profile of v2, /device:TPU:8, one launch (start us, length us, event | category | flops | bytes accessed | tf_op | source)
XLA Modules:
  0.0 146.0 jit_solution(4617178088493583749)
XLA Ops:
  0.0 0.9 copy.114
  0.9 0.8 broadcast_in_dim.104
  1.7 8.5 %all-to-all-start = ((bf16[8,16,1536]{2,1,0:T(8,128)(2,1)}), bf16[8,16,1536]{2,1,0:T(8,128)(2,1)S(1)}, u32[]{:S(2)}, u32[]{:S(2)}) async-start(bf16[8,16,1536]{2,1,0:T(8,128)(2,1)} %broadcast_in_dim.104), calls=%async_computation | async-start | bytes 786432 | tf_op jit(solution)/shard_map/all_to_all | solution.py:20
  10.1 1.3 compare_reduce_fusion.1
  11.8 0.5 fusion.73
  13.4 0.5 collective-permute-start.4
  13.9 2.6 %collective-permute-start.5 = (bf16[16,1536]{1,0:T(8,128)(2,1)S(1)}, bf16[16,1536]{1,0:T(8,128)(2,1)S(1)}, u32[]{:S(2)}, u32[]{:S(2)}) collective-permute-start(bf16[16,1536]{1,0:T(8,128)(2,1)S(1)} %get-tuple-element.714), channel_id=1, source_target_pairs={{2,0},{3,1},{0,2},{1,3},{6,4},{7,5},{4,6},{5,7},{10,8},{11,9},{8,1... | collective-permute-start | bytes 147464 | tf_op jit(solution)/shard_map/ppermute | solution.py:35
  16.5 1.9 %collective-permute-start.6 = (bf16[16,1536]{1,0:T(8,128)(2,1)S(1)}, bf16[16,1536]{1,0:T(8,128)(2,1)S(1)}, u32[]{:S(2)}, u32[]{:S(2)}) collective-permute-start(bf16[16,1536]{1,0:T(8,128)(2,1)S(1)} %get-tuple-element.714), channel_id=1, source_target_pairs={{3,0},{0,1},{1,2},{2,3},{7,4},{4,5},{5,6},{6,7},{11,8},{8,9},{9,10... | collective-permute-start | bytes 147464 | tf_op jit(solution)/shard_map/ppermute | solution.py:35
  18.4 1.1 collective-permute-done.5
  19.5 1.1 collective-permute-done.6
  20.6 4.2 %all-to-all-done = bf16[8,16,1536]{2,1,0:T(8,128)(2,1)S(1)} async-done(((bf16[8,16,1536]{2,1,0:T(8,128)(2,1)}), bf16[8,16,1536]{2,1,0:T(8,128)(2,1)S(1)}, u32[]{:S(2)}, u32[]{:S(2)}) %all-to-all-start) | async-done | bytes 393248 | tf_op jit(solution)/shard_map/all_to_all | solution.py:20
  24.8 1.4 broadcast_in_dim.105
  26.2 4.9 %all-to-all-start.1 = ((bf16[4,8,16,1536]{3,2,1,0:T(8,128)(2,1)}), bf16[4,8,16,1536]{3,2,1,0:T(8,128)(2,1)S(1)}, u32[]{:S(2)}, u32[]{:S(2)}) async-start(bf16[4,8,16,1536]{3,2,1,0:T(8,128)(2,1)} %broadcast_in_dim.105), calls=%async_computation.1 | async-start | bytes 3145728 | tf_op jit(solution)/shard_map/all_to_all | solution.py:20
  31.2 1.9 %collective-permute-start.12 = (bf16[4,16,1536]{2,1,0:T(8,128)(2,1)S(1)}, bf16[4,16,1536]{2,1,0:T(8,128)(2,1)S(1)}, u32[]{:S(2)}, u32[]{:S(2)}) collective-permute-start(bf16[4,16,1536]{2,1,0:T(8,128)(2,1)S(1)} %pad_maximum_fusion.2), channel_id=1, source_target_pairs={{28,0},{0,4},{4,8},{8,12},{12,16},{16,20},{20,24},{24,28},{29,1},{... | collective-permute-start | bytes 589832 | tf_op jit(solution)/shard_map/ppermute | solution.py:35
  33.1 3.6 %collective-permute-done.7 = bf16[4,16,1536]{2,1,0:T(8,128)(2,1)S(1)} collective-permute-done((bf16[4,16,1536]{2,1,0:T(8,128)(2,1)S(1)}, bf16[4,16,1536]{2,1,0:T(8,128)(2,1)S(1)}, u32[]{:S(2)}, u32[]{:S(2)}) %collective-permute-start.7) | collective-permute-done | bytes 196640 | tf_op jit(solution)/shard_map/ppermute | solution.py:35
  36.8 1.4 collective-permute-start.8
  38.1 0.7 collective-permute-start.13
  38.8 4.2 %collective-permute-done.8 = bf16[4,16,1536]{2,1,0:T(8,128)(2,1)S(1)} collective-permute-done((bf16[4,16,1536]{2,1,0:T(8,128)(2,1)S(1)}, bf16[4,16,1536]{2,1,0:T(8,128)(2,1)S(1)}, u32[]{:S(2)}, u32[]{:S(2)}) %collective-permute-start.8) | collective-permute-done | bytes 196640 | tf_op jit(solution)/shard_map/ppermute | solution.py:35
  43.0 2.0 %collective-permute-start.9 = (bf16[4,16,1536]{2,1,0:T(8,128)(2,1)S(1)}, bf16[4,16,1536]{2,1,0:T(8,128)(2,1)S(1)}, u32[]{:S(2)}, u32[]{:S(2)}) collective-permute-start(bf16[4,16,1536]{2,1,0:T(8,128)(2,1)S(1)} %collective-permute-done.8), channel_id=1, source_target_pairs={{4,0},{8,4},{12,8},{16,12},{20,16},{24,20},{28,24},{0,28},{5,1},{9... | collective-permute-start | bytes 589832 | tf_op jit(solution)/shard_map/ppermute | solution.py:35
  45.1 0.5 collective-permute-start.14
  45.6 3.5 %collective-permute-done.9 = bf16[4,16,1536]{2,1,0:T(8,128)(2,1)S(1)} collective-permute-done((bf16[4,16,1536]{2,1,0:T(8,128)(2,1)S(1)}, bf16[4,16,1536]{2,1,0:T(8,128)(2,1)S(1)}, u32[]{:S(2)}, u32[]{:S(2)}) %collective-permute-start.9) | collective-permute-done | bytes 196640 | tf_op jit(solution)/shard_map/ppermute | solution.py:35
  49.0 0.6 all-to-all-done.1
  49.6 2.6 %collective-permute-start.11 = (bf16[4,16,1536]{2,1,0:T(8,128)(2,1)S(1)}, bf16[4,16,1536]{2,1,0:T(8,128)(2,1)S(1)}, u32[]{:S(2)}, u32[]{:S(2)}) collective-permute-start(bf16[4,16,1536]{2,1,0:T(8,128)(2,1)S(1)} %collective-permute-done.9), channel_id=1, source_target_pairs={{4,0},{8,4},{12,8},{16,12},{20,16},{24,20},{28,24},{0,28},{5,1},{9... | collective-permute-start | bytes 589832 | tf_op jit(solution)/shard_map/ppermute | solution.py:35
  52.2 6.0 %shard_map.57 = bf16[8,192,128]{2,1,0:T(8,128)(2,1)S(1)} custom-call(s32[8]{0:T(128)S(1)} %stack.65.at_ref, bf16[512,1536]{1,0:T(8,128)(2,1)S(1)} %bitcast.156, bf16[12,1536,128]{2,1,0:T(8,128)(2,1)} %refs_8_.1, f32[3,4,128]{2,1,0:T(4,128)S(1)} %reshape.215.refs_2_.refs_9_, s32[3,16,256]{2,1,0:T(8,128)S(1)} %reshape.213.refs_3_.refs_10_.pos_ref), custom_call_target="tpu_custom_call" | custom-call | flops 4831838208 | bytes 9437184 | tf_op jit(solution)/shard_map/pallas_call | solution.py:95
  58.7 4.5 %shard_map.58 = bf16[8,192,128]{2,1,0:T(8,128)(2,1)S(1)} custom-call(s32[8]{0:T(128)S(1)} %stack.65.at_ref, bf16[64,1536]{1,0:T(8,128)(2,1)S(1)} %bitcast.157, bf16[64,1536]{1,0:T(8,128)(2,1)S(1)} %bitcast.158, bf16[64,1536]{1,0:T(8,128)(2,1)S(1)} %bitcast.160, bf16[64,1536]{1,0:T(8,128)(2,1)S(1)} %bitcast.162, bf16[64,1536]{1,0:T(8,128)(2,1)S(1)} %bitcast.164, ...), custom_call_target="tpu_custom_call" | custom-call | flops 4831838208 | bytes 9437184 | tf_op jit(solution)/shard_map/pallas_call | solution.py:95
  63.2 0.6 collective-permute-start.15
  63.8 1.0 collective-permute-done.15
  64.9 1.6 %collective-permute-start.16 = (bf16[384,128]{1,0:T(8,128)(2,1)S(1)}, bf16[384,128]{1,0:T(8,128)(2,1)S(1)}, u32[]{:S(2)}, u32[]{:S(2)}) collective-permute-start(bf16[384,128]{1,0:T(8,128)(2,1)S(1)} %get-tuple-element.850), channel_id=1, source_target_pairs={{192,0},{0,64},{64,128},{128,192},{193,1},{1,65},{65,129},{129,193... | collective-permute-start | bytes 294920 | tf_op jit(solution)/shard_map/ppermute | solution.py:35
  66.5 2.7 %collective-permute-start.17 = (bf16[384,128]{1,0:T(8,128)(2,1)S(1)}, bf16[384,128]{1,0:T(8,128)(2,1)S(1)}, u32[]{:S(2)}, u32[]{:S(2)}) collective-permute-start(bf16[384,128]{1,0:T(8,128)(2,1)S(1)} %get-tuple-element.852), channel_id=1, source_target_pairs={{128,0},{192,64},{0,128},{64,192},{129,1},{193,65},{1,129},{65,193... | collective-permute-start | bytes 294920 | tf_op jit(solution)/shard_map/ppermute | solution.py:35
  69.2 1.5 %collective-permute-start.18 = (bf16[384,128]{1,0:T(8,128)(2,1)S(1)}, bf16[384,128]{1,0:T(8,128)(2,1)S(1)}, u32[]{:S(2)}, u32[]{:S(2)}) collective-permute-start(bf16[384,128]{1,0:T(8,128)(2,1)S(1)} %get-tuple-element.851), channel_id=1, source_target_pairs={{64,0},{128,64},{192,128},{0,192},{65,1},{129,65},{193,129},{1,193... | collective-permute-start | bytes 294920 | tf_op jit(solution)/shard_map/ppermute | solution.py:35
  70.7 0.6 collective-permute-done.16
  71.3 3.1 %collective-permute-done.17 = bf16[384,128]{1,0:T(8,128)(2,1)S(1)} collective-permute-done((bf16[384,128]{1,0:T(8,128)(2,1)S(1)}, bf16[384,128]{1,0:T(8,128)(2,1)S(1)}, u32[]{:S(2)}, u32[]{:S(2)}) %collective-permute-start.17) | collective-permute-done | bytes 98336 | tf_op jit(solution)/shard_map/ppermute | solution.py:35
  74.4 2.4 %collective-permute-start.19 = (bf16[384,128]{1,0:T(8,128)(2,1)S(1)}, bf16[384,128]{1,0:T(8,128)(2,1)S(1)}, u32[]{:S(2)}, u32[]{:S(2)}) collective-permute-start(bf16[384,128]{1,0:T(8,128)(2,1)S(1)} %get-tuple-element.841), channel_id=1, source_target_pairs={{64,0},{128,64},{192,128},{0,192},{65,1},{129,65},{193,129},{1,193... | collective-permute-start | bytes 294920 | tf_op jit(solution)/shard_map/ppermute | solution.py:35
  76.8 1.1 collective-permute-start.20
  77.9 0.7 collective-permute-start.21
  78.8 1.9 %collective-permute-done.19 = bf16[384,128]{1,0:T(8,128)(2,1)S(1)} collective-permute-done((bf16[384,128]{1,0:T(8,128)(2,1)S(1)}, bf16[384,128]{1,0:T(8,128)(2,1)S(1)}, u32[]{:S(2)}, u32[]{:S(2)}) %collective-permute-start.19) | collective-permute-done | bytes 98336 | tf_op jit(solution)/shard_map/ppermute | solution.py:35
  80.7 2.2 %collective-permute-done.20 = bf16[384,128]{1,0:T(8,128)(2,1)S(1)} collective-permute-done((bf16[384,128]{1,0:T(8,128)(2,1)S(1)}, bf16[384,128]{1,0:T(8,128)(2,1)S(1)}, u32[]{:S(2)}, u32[]{:S(2)}) %collective-permute-start.20) | collective-permute-done | bytes 98336 | tf_op jit(solution)/shard_map/ppermute | solution.py:35
  82.9 1.0 collective-permute-done.21
  84.2 1.6 %collective-permute-done.22 = bf16[4,384,128]{2,1,0:T(8,128)(2,1)S(1)} collective-permute-done((bf16[4,384,128]{2,1,0:T(8,128)(2,1)S(1)}, bf16[4,384,128]{2,1,0:T(8,128)(2,1)S(1)}, u32[]{:S(2)}, u32[]{:S(2)}) %collective-permute-start.22) | collective-permute-done | bytes 393248 | tf_op jit(solution)/shard_map/ppermute | solution.py:35
  85.9 5.1 %shard_map.60 = bf16[512,1536]{1,0:T(8,128)(2,1)S(1)} custom-call(s32[8]{0:T(128)S(1)} %stack.65.at_ref, bf16[8,384,128]{2,1,0:T(8,128)(2,1)S(1)} %constant_dynamic-update-slice_fusion.2.packed_ref, s32[3,16,256]{2,1,0:T(8,128)S(1)} %reshape.213.refs_3_.refs_10_.pos_ref, bf16[12,128,1536]{2,1,0:T(8,128)(2,1)S(1)} %bitcast.176), custom_call_target="tpu_custom_call" | custom-call | flops 2415919104 | bytes 7340032 | tf_op jit(solution)/shard_map/pallas_call | solution.py:145
  91.0 1.0 fusion.72
  91.9 0.8 collective-permute-start.23
  92.8 1.2 collective-permute-start.27
  94.0 5.8 %shard_map.59 = bf16[512,1536]{1,0:T(8,128)(2,1)} custom-call(s32[8]{0:T(128)S(1)} %stack.65.at_ref, bf16[8,384,128]{2,1,0:T(8,128)(2,1)S(1)} %constant_dynamic-update-slice_fusion.2.packed_ref, s32[3,16,256]{2,1,0:T(8,128)S(1)} %reshape.213.refs_3_.refs_10_.pos_ref, bf16[12,128,1536]{2,1,0:T(8,128)(2,1)S(1)} %bitcast.176), custom_call_target="tpu_custom_call" | custom-call | flops 2415919104 | bytes 7340032 | tf_op jit(solution)/shard_map/pallas_call | solution.py:145
  99.8 5.5 %all-to-all-start.2 = ((bf16[4,8,16,1536]{3,2,1,0:T(8,128)(2,1)}), bf16[4,8,16,1536]{3,2,1,0:T(8,128)(2,1)S(1)}, u32[]{:S(2)}, u32[]{:S(2)}) async-start(bf16[4,8,16,1536]{3,2,1,0:T(8,128)(2,1)} %bitcast.44), calls=%async_computation.2 | async-start | bytes 3145728 | tf_op jit(solution)/shard_map/all_to_all | solution.py:26
  105.3 1.0 fusion.10
  106.2 2.3 %collective-permute-start.24 = (bf16[4,16,1536]{2,1,0:T(8,128)(2,1)S(1)}, bf16[4,16,1536]{2,1,0:T(8,128)(2,1)S(1)}, u32[]{:S(2)}, u32[]{:S(2)}) collective-permute-start(bf16[4,16,1536]{2,1,0:T(8,128)(2,1)S(1)} %fusion.10), channel_id=1, source_target_pairs={{4,0},{8,4},{12,8},{16,12},{20,16},{24,20},{28,24},{0,28},{5,1},{9... | collective-permute-start | bytes 589832 | tf_op jit(solution)/shard_map/ppermute | solution.py:35
  108.5 1.0 fusion.8
  109.6 2.7 %collective-permute-done.24 = bf16[4,16,1536]{2,1,0:T(8,128)(2,1)S(1)} collective-permute-done((bf16[4,16,1536]{2,1,0:T(8,128)(2,1)S(1)}, bf16[4,16,1536]{2,1,0:T(8,128)(2,1)S(1)}, u32[]{:S(2)}, u32[]{:S(2)}) %collective-permute-start.24) | collective-permute-done | bytes 196640 | tf_op jit(solution)/shard_map/ppermute | solution.py:35
  112.4 3.3 %collective-permute-start.25 = (bf16[4,16,1536]{2,1,0:T(8,128)(2,1)S(1)}, bf16[4,16,1536]{2,1,0:T(8,128)(2,1)S(1)}, u32[]{:S(2)}, u32[]{:S(2)}) collective-permute-start(bf16[4,16,1536]{2,1,0:T(8,128)(2,1)S(1)} %fusion.11), channel_id=1, source_target_pairs={{4,0},{8,4},{12,8},{16,12},{20,16},{24,20},{28,24},{0,28},{5,1},{9... | collective-permute-start | bytes 589832 | tf_op jit(solution)/shard_map/ppermute | solution.py:35
  115.7 0.8 collective-permute-done.28
  116.6 2.3 %collective-permute-done.25 = bf16[4,16,1536]{2,1,0:T(8,128)(2,1)S(1)} collective-permute-done((bf16[4,16,1536]{2,1,0:T(8,128)(2,1)S(1)}, bf16[4,16,1536]{2,1,0:T(8,128)(2,1)S(1)}, u32[]{:S(2)}, u32[]{:S(2)}) %collective-permute-start.25) | collective-permute-done | bytes 196640 | tf_op jit(solution)/shard_map/ppermute | solution.py:35
  118.9 3.8 %collective-permute-start.26 = (bf16[4,16,1536]{2,1,0:T(8,128)(2,1)S(1)}, bf16[4,16,1536]{2,1,0:T(8,128)(2,1)S(1)}, u32[]{:S(2)}, u32[]{:S(2)}) collective-permute-start(bf16[4,16,1536]{2,1,0:T(8,128)(2,1)S(1)} %fusion.12), channel_id=1, source_target_pairs={{4,0},{8,4},{12,8},{16,12},{20,16},{24,20},{28,24},{0,28},{5,1},{9... | collective-permute-start | bytes 589832 | tf_op jit(solution)/shard_map/ppermute | solution.py:35
  122.7 0.9 convert_reduce_fusion
  123.6 2.3 %collective-permute-done.26 = bf16[4,16,1536]{2,1,0:T(8,128)(2,1)S(1)} collective-permute-done((bf16[4,16,1536]{2,1,0:T(8,128)(2,1)S(1)}, bf16[4,16,1536]{2,1,0:T(8,128)(2,1)S(1)}, u32[]{:S(2)}, u32[]{:S(2)}) %collective-permute-start.26) | collective-permute-done | bytes 196640 | tf_op jit(solution)/shard_map/ppermute | solution.py:35
  126.0 1.1 reduce_sum.47
  127.0 6.4 %all-to-all-start.3 = ((bf16[8,16,1536]{2,1,0:T(8,128)(2,1)}), bf16[8,16,1536]{2,1,0:T(8,128)(2,1)S(1)}, u32[]{:S(2)}, u32[]{:S(2)}) async-start(bf16[8,16,1536]{2,1,0:T(8,128)(2,1)} %reduce_sum.47), calls=%async_computation.3 | async-start | bytes 786432 | tf_op jit(solution)/shard_map/all_to_all | solution.py:26
  133.4 1.5 %collective-permute-start.30 = (bf16[16,1536]{1,0:T(8,128)(2,1)S(1)}, bf16[16,1536]{1,0:T(8,128)(2,1)S(1)}, u32[]{:S(2)}, u32[]{:S(2)}) collective-permute-start(bf16[16,1536]{1,0:T(8,128)(2,1)S(1)} %get-tuple-element.853), channel_id=1, source_target_pairs={{3,0},{0,1},{1,2},{2,3},{7,4},{4,5},{5,6},{6,7},{11,8},{8,9},{9,10... | collective-permute-start | bytes 147464 | tf_op jit(solution)/shard_map/ppermute | solution.py:35
  135.0 0.9 collective-permute-start.31
  135.9 2.3 %collective-permute-start.32 = (bf16[16,1536]{1,0:T(8,128)(2,1)S(1)}, bf16[16,1536]{1,0:T(8,128)(2,1)S(1)}, u32[]{:S(2)}, u32[]{:S(2)}) collective-permute-start(bf16[16,1536]{1,0:T(8,128)(2,1)S(1)} %get-tuple-element.854), channel_id=1, source_target_pairs={{1,0},{2,1},{3,2},{0,3},{5,4},{6,5},{7,6},{4,7},{9,8},{10,9},{11,1... | collective-permute-start | bytes 147464 | tf_op jit(solution)/shard_map/ppermute | solution.py:35
  138.2 1.0 convolution_reduce_fusion
  139.9 0.7 collective-permute-done.31
  140.6 4.7 %all-to-all-done.3 = bf16[8,16,1536]{2,1,0:T(8,128)(2,1)S(1)} async-done(((bf16[8,16,1536]{2,1,0:T(8,128)(2,1)}), bf16[8,16,1536]{2,1,0:T(8,128)(2,1)S(1)}, u32[]{:S(2)}, u32[]{:S(2)}) %all-to-all-start.3) | async-done | bytes 393248 | tf_op jit(solution)/shard_map/all_to_all | solution.py:26
  145.4 0.6 pad_maximum_fusion.3
  (81 shorter events, 3.1 us)
Async XLA Ops:
  1.7 23.2 %all-to-all-start = ((bf16[8,16,1536]{2,1,0:T(8,128)(2,1)}), bf16[8,16,1536]{2,1,0:T(8,128)(2,1)S(1)}, u32[]{:S(2)}, u32[]{:S(2)}) async-start(bf16[8,16,1536]{2,1,0:T(8,128)(2,1)} %broadcast_in_dim.104), calls=%async_computation | async-start | bytes 786432 | tf_op jit(solution)/shard_map/all_to_all | solution.py:20
  13.2 31.8 %copy-start.5 = (f32[12,128]{1,0:T(8,128)S(1)}, f32[12,128]{1,0:T(8,128)}, u32[]{:S(2)}) copy-start(f32[12,128]{1,0:T(8,128)} %param.20) | copy-start | bytes 18436
  13.4 5.0 %collective-permute-start.4 = (bf16[16,1536]{1,0:T(8,128)(2,1)S(1)}, bf16[16,1536]{1,0:T(8,128)(2,1)S(1)}, u32[]{:S(2)}, u32[]{:S(2)}) collective-permute-start(bf16[16,1536]{1,0:T(8,128)(2,1)S(1)} %get-tuple-element.714), channel_id=1, source_target_pairs={{1,0},{2,1},{3,2},{0,3},{5,4},{6,5},{7,6},{4,7},{9,8},{10,9},{11,1... | collective-permute-start | bytes 147464 | tf_op jit(solution)/shard_map/ppermute | solution.py:35
  13.9 5.6 %collective-permute-start.5 = (bf16[16,1536]{1,0:T(8,128)(2,1)S(1)}, bf16[16,1536]{1,0:T(8,128)(2,1)S(1)}, u32[]{:S(2)}, u32[]{:S(2)}) collective-permute-start(bf16[16,1536]{1,0:T(8,128)(2,1)S(1)} %get-tuple-element.714), channel_id=1, source_target_pairs={{2,0},{3,1},{0,2},{1,3},{6,4},{7,5},{4,6},{5,7},{10,8},{11,9},{8,1... | collective-permute-start | bytes 147464 | tf_op jit(solution)/shard_map/ppermute | solution.py:35
  16.5 4.1 %collective-permute-start.6 = (bf16[16,1536]{1,0:T(8,128)(2,1)S(1)}, bf16[16,1536]{1,0:T(8,128)(2,1)S(1)}, u32[]{:S(2)}, u32[]{:S(2)}) collective-permute-start(bf16[16,1536]{1,0:T(8,128)(2,1)S(1)} %get-tuple-element.714), channel_id=1, source_target_pairs={{3,0},{0,1},{1,2},{2,3},{7,4},{4,5},{5,6},{6,7},{11,8},{8,9},{9,10... | collective-permute-start | bytes 147464 | tf_op jit(solution)/shard_map/ppermute | solution.py:35
  26.2 23.4 %all-to-all-start.1 = ((bf16[4,8,16,1536]{3,2,1,0:T(8,128)(2,1)}), bf16[4,8,16,1536]{3,2,1,0:T(8,128)(2,1)S(1)}, u32[]{:S(2)}, u32[]{:S(2)}) async-start(bf16[4,8,16,1536]{3,2,1,0:T(8,128)(2,1)} %broadcast_in_dim.105), calls=%async_computation.1 | async-start | bytes 3145728 | tf_op jit(solution)/shard_map/all_to_all | solution.py:20
  31.1 5.7 %collective-permute-start.7 = (bf16[4,16,1536]{2,1,0:T(8,128)(2,1)S(1)}, bf16[4,16,1536]{2,1,0:T(8,128)(2,1)S(1)}, u32[]{:S(2)}, u32[]{:S(2)}) collective-permute-start(bf16[4,16,1536]{2,1,0:T(8,128)(2,1)S(1)} %pad_maximum_fusion.2), channel_id=1, source_target_pairs={{4,0},{8,4},{12,8},{16,12},{20,16},{24,20},{28,24},{0,28},{5,1},{9... | collective-permute-start | bytes 589832 | tf_op jit(solution)/shard_map/ppermute | solution.py:35
  31.2 6.9 %collective-permute-start.12 = (bf16[4,16,1536]{2,1,0:T(8,128)(2,1)S(1)}, bf16[4,16,1536]{2,1,0:T(8,128)(2,1)S(1)}, u32[]{:S(2)}, u32[]{:S(2)}) collective-permute-start(bf16[4,16,1536]{2,1,0:T(8,128)(2,1)S(1)} %pad_maximum_fusion.2), channel_id=1, source_target_pairs={{28,0},{0,4},{4,8},{8,12},{12,16},{16,20},{20,24},{24,28},{29,1},{... | collective-permute-start | bytes 589832 | tf_op jit(solution)/shard_map/ppermute | solution.py:35
  36.8 6.2 %collective-permute-start.8 = (bf16[4,16,1536]{2,1,0:T(8,128)(2,1)S(1)}, bf16[4,16,1536]{2,1,0:T(8,128)(2,1)S(1)}, u32[]{:S(2)}, u32[]{:S(2)}) collective-permute-start(bf16[4,16,1536]{2,1,0:T(8,128)(2,1)S(1)} %collective-permute-done.7), channel_id=1, source_target_pairs={{4,0},{8,4},{12,8},{16,12},{20,16},{24,20},{28,24},{0,28},{5,1},{9... | collective-permute-start | bytes 589832 | tf_op jit(solution)/shard_map/ppermute | solution.py:35
  38.1 7.0 %collective-permute-start.13 = (bf16[4,16,1536]{2,1,0:T(8,128)(2,1)S(1)}, bf16[4,16,1536]{2,1,0:T(8,128)(2,1)S(1)}, u32[]{:S(2)}, u32[]{:S(2)}) collective-permute-start(bf16[4,16,1536]{2,1,0:T(8,128)(2,1)S(1)} %collective-permute-done.12), channel_id=1, source_target_pairs={{28,0},{0,4},{4,8},{8,12},{12,16},{16,20},{20,24},{24,28},{29,1},{... | collective-permute-start | bytes 589832 | tf_op jit(solution)/shard_map/ppermute | solution.py:35
  43.0 6.0 %collective-permute-start.9 = (bf16[4,16,1536]{2,1,0:T(8,128)(2,1)S(1)}, bf16[4,16,1536]{2,1,0:T(8,128)(2,1)S(1)}, u32[]{:S(2)}, u32[]{:S(2)}) collective-permute-start(bf16[4,16,1536]{2,1,0:T(8,128)(2,1)S(1)} %collective-permute-done.8), channel_id=1, source_target_pairs={{4,0},{8,4},{12,8},{16,12},{20,16},{24,20},{28,24},{0,28},{5,1},{9... | collective-permute-start | bytes 589832 | tf_op jit(solution)/shard_map/ppermute | solution.py:35
  45.1 13.5 %collective-permute-start.14 = (bf16[4,16,1536]{2,1,0:T(8,128)(2,1)S(1)}, bf16[4,16,1536]{2,1,0:T(8,128)(2,1)S(1)}, u32[]{:S(2)}, u32[]{:S(2)}) collective-permute-start(bf16[4,16,1536]{2,1,0:T(8,128)(2,1)S(1)} %collective-permute-done.13), channel_id=1, source_target_pairs={{28,0},{0,4},{4,8},{8,12},{12,16},{16,20},{20,24},{24,28},{29,1},{... | collective-permute-start | bytes 589832 | tf_op jit(solution)/shard_map/ppermute | solution.py:35
  49.6 9.0 %slice-start = ((s8[4718592]{0:T(1024)(128)(4,1)}), s8[4194304]{0:T(1024)(128)(4,1)S(1)}, s32[]{:S(2)}) async-start(s8[4718592]{0:T(1024)(128)(4,1)} %bitcast.173), calls=%async_computation.4 | async-start | bytes 8388608
  49.6 9.1 %slice-start.1 = ((s8[4718592]{0:T(1024)(128)(4,1)}), s8[524288]{0:T(1024)(128)(4,1)S(1)}, s32[]{:S(2)}) async-start(s8[4718592]{0:T(1024)(128)(4,1)} %bitcast.173), calls=%async_computation.5 | async-start | bytes 1048576
  49.6 9.0 %collective-permute-start.11 = (bf16[4,16,1536]{2,1,0:T(8,128)(2,1)S(1)}, bf16[4,16,1536]{2,1,0:T(8,128)(2,1)S(1)}, u32[]{:S(2)}, u32[]{:S(2)}) collective-permute-start(bf16[4,16,1536]{2,1,0:T(8,128)(2,1)S(1)} %collective-permute-done.9), channel_id=1, source_target_pairs={{4,0},{8,4},{12,8},{16,12},{20,16},{24,20},{28,24},{0,28},{5,1},{9... | collective-permute-start | bytes 589832 | tf_op jit(solution)/shard_map/ppermute | solution.py:35
  58.3 5.4 %collective-permute-start.10 = (bf16[4,192,128]{2,1,0:T(8,128)(2,1)S(1)}, bf16[4,192,128]{2,1,0:T(8,128)(2,1)S(1)}, u32[]{:S(2)}, u32[]{:S(2)}) collective-permute-start(bf16[4,192,128]{2,1,0:T(8,128)(2,1)S(1)} %slice.107), channel_id=1, source_target_pairs={{32,0},{0,32},{33,1},{1,33},{34,2},{2,34},{35,3},{3,35},{36,4},{4,... | collective-permute-start | bytes 589832 | tf_op jit(solution)/shard_map/ppermute | solution.py:35
  58.6 27.3 %slice-start.2 = ((s8[4718592]{0:T(1024)(128)(4,1)}), s8[4194304]{0:T(1024)(128)(4,1)S(1)}, s32[]{:S(2)}) async-start(s8[4718592]{0:T(1024)(128)(4,1)} %bitcast.175), calls=%async_computation.6 | async-start | bytes 8388608
  58.7 27.3 %slice-start.3 = ((s8[4718592]{0:T(1024)(128)(4,1)}), s8[524288]{0:T(1024)(128)(4,1)S(1)}, s32[]{:S(2)}) async-start(s8[4718592]{0:T(1024)(128)(4,1)} %bitcast.175), calls=%async_computation.7 | async-start | bytes 1048576
  63.1 15.5 %copy-start.1 = (s32[1024,48]{0,1:T(8,128)S(1)}, s32[1024,48]{0,1:T(8,128)}, u32[]{:S(2)}) copy-start(s32[1024,48]{0,1:T(8,128)} %param.18) | copy-start | bytes 589828
  63.2 1.6 %collective-permute-start.15 = (bf16[4,192,128]{2,1,0:T(8,128)(2,1)S(1)}, bf16[4,192,128]{2,1,0:T(8,128)(2,1)S(1)}, u32[]{:S(2)}, u32[]{:S(2)}) collective-permute-start(bf16[4,192,128]{2,1,0:T(8,128)(2,1)S(1)} %slice.109), channel_id=1, source_target_pairs={{32,0},{0,32},{33,1},{1,33},{34,2},{2,34},{35,3},{3,35},{36,4},{4,... | collective-permute-start | bytes 589832 | tf_op jit(solution)/shard_map/ppermute | solution.py:35
  64.9 6.4 %collective-permute-start.16 = (bf16[384,128]{1,0:T(8,128)(2,1)S(1)}, bf16[384,128]{1,0:T(8,128)(2,1)S(1)}, u32[]{:S(2)}, u32[]{:S(2)}) collective-permute-start(bf16[384,128]{1,0:T(8,128)(2,1)S(1)} %get-tuple-element.850), channel_id=1, source_target_pairs={{192,0},{0,64},{64,128},{128,192},{193,1},{1,65},{65,129},{129,193... | collective-permute-start | bytes 294920 | tf_op jit(solution)/shard_map/ppermute | solution.py:35
  66.5 7.9 %collective-permute-start.17 = (bf16[384,128]{1,0:T(8,128)(2,1)S(1)}, bf16[384,128]{1,0:T(8,128)(2,1)S(1)}, u32[]{:S(2)}, u32[]{:S(2)}) collective-permute-start(bf16[384,128]{1,0:T(8,128)(2,1)S(1)} %get-tuple-element.852), channel_id=1, source_target_pairs={{128,0},{192,64},{0,128},{64,192},{129,1},{193,65},{1,129},{65,193... | collective-permute-start | bytes 294920 | tf_op jit(solution)/shard_map/ppermute | solution.py:35
  69.2 5.1 %collective-permute-start.18 = (bf16[384,128]{1,0:T(8,128)(2,1)S(1)}, bf16[384,128]{1,0:T(8,128)(2,1)S(1)}, u32[]{:S(2)}, u32[]{:S(2)}) collective-permute-start(bf16[384,128]{1,0:T(8,128)(2,1)S(1)} %get-tuple-element.851), channel_id=1, source_target_pairs={{64,0},{128,64},{192,128},{0,192},{65,1},{129,65},{193,129},{1,193... | collective-permute-start | bytes 294920 | tf_op jit(solution)/shard_map/ppermute | solution.py:35
  74.4 6.3 %collective-permute-start.19 = (bf16[384,128]{1,0:T(8,128)(2,1)S(1)}, bf16[384,128]{1,0:T(8,128)(2,1)S(1)}, u32[]{:S(2)}, u32[]{:S(2)}) collective-permute-start(bf16[384,128]{1,0:T(8,128)(2,1)S(1)} %get-tuple-element.841), channel_id=1, source_target_pairs={{64,0},{128,64},{192,128},{0,192},{65,1},{129,65},{193,129},{1,193... | collective-permute-start | bytes 294920 | tf_op jit(solution)/shard_map/ppermute | solution.py:35
  76.8 6.2 %collective-permute-start.20 = (bf16[384,128]{1,0:T(8,128)(2,1)S(1)}, bf16[384,128]{1,0:T(8,128)(2,1)S(1)}, u32[]{:S(2)}, u32[]{:S(2)}) collective-permute-start(bf16[384,128]{1,0:T(8,128)(2,1)S(1)} %get-tuple-element.841), channel_id=1, source_target_pairs={{128,0},{192,64},{0,128},{64,192},{129,1},{193,65},{1,129},{65,193... | collective-permute-start | bytes 294920 | tf_op jit(solution)/shard_map/ppermute | solution.py:35
  77.9 6.0 %collective-permute-start.21 = (bf16[384,128]{1,0:T(8,128)(2,1)S(1)}, bf16[384,128]{1,0:T(8,128)(2,1)S(1)}, u32[]{:S(2)}, u32[]{:S(2)}) collective-permute-start(bf16[384,128]{1,0:T(8,128)(2,1)S(1)} %get-tuple-element.841), channel_id=1, source_target_pairs={{192,0},{0,64},{64,128},{128,192},{193,1},{1,65},{65,129},{129,193... | collective-permute-start | bytes 294920 | tf_op jit(solution)/shard_map/ppermute | solution.py:35
  84.0 1.8 %collective-permute-start.22 = (bf16[4,384,128]{2,1,0:T(8,128)(2,1)S(1)}, bf16[4,384,128]{2,1,0:T(8,128)(2,1)S(1)}, u32[]{:S(2)}, u32[]{:S(2)}) collective-permute-start(bf16[4,384,128]{2,1,0:T(8,128)(2,1)S(1)} %pad_maximum_fusion.1), channel_id=1, source_target_pairs={{32,0},{0,32},{33,1},{1,33},{34,2},{2,34},{35,3},{3,35},{36,4},{4,... | collective-permute-start | bytes 1179656 | tf_op jit(solution)/shard_map/ppermute | solution.py:35
  91.9 13.3 %collective-permute-start.23 = (bf16[4,16,1536]{2,1,0:T(8,128)(2,1)}, bf16[4,16,1536]{2,1,0:T(8,128)(2,1)}, u32[]{:S(2)}, u32[]{:S(2)}) collective-permute-start(bf16[4,16,1536]{2,1,0:T(8,128)(2,1)} %bitcast.49), channel_id=1, source_target_pairs={{4,0},{8,4},{12,8},{16,12},{20,16},{24,20},{28,24},{0,28},{5,1},{9... | collective-permute-start | bytes 589832 | tf_op jit(solution)/shard_map/ppermute | solution.py:35
  92.8 15.8 %collective-permute-start.27 = (bf16[4,16,1536]{2,1,0:T(8,128)(2,1)}, bf16[4,16,1536]{2,1,0:T(8,128)(2,1)}, u32[]{:S(2)}, u32[]{:S(2)}) collective-permute-start(bf16[4,16,1536]{2,1,0:T(8,128)(2,1)} %bitcast.52), channel_id=1, source_target_pairs={{28,0},{0,4},{4,8},{8,12},{12,16},{16,20},{20,24},{24,28},{29,1},{... | collective-permute-start | bytes 589832 | tf_op jit(solution)/shard_map/ppermute | solution.py:35
  99.8 5.5 %copy-start.4 = (bf16[64,1536]{1,0:T(8,128)(2,1)S(1)}, bf16[64,1536]{1,0:T(8,128)(2,1)}, u32[]{:S(2)}) copy-start(bf16[64,1536]{1,0:T(8,128)(2,1)} %get-tuple-element.846) | copy-start | bytes 589828
  99.8 8.7 %copy-start.3 = (bf16[64,1536]{1,0:T(8,128)(2,1)S(1)}, bf16[64,1536]{1,0:T(8,128)(2,1)}, u32[]{:S(2)}) copy-start(bf16[64,1536]{1,0:T(8,128)(2,1)} %get-tuple-element.844) | copy-start | bytes 589828
  99.8 12.6 %copy-start.2 = (bf16[64,1536]{1,0:T(8,128)(2,1)S(1)}, bf16[64,1536]{1,0:T(8,128)(2,1)}, u32[]{:S(2)}) copy-start(bf16[64,1536]{1,0:T(8,128)(2,1)} %get-tuple-element.847) | copy-start | bytes 589828
  99.8 26.2 %all-to-all-start.2 = ((bf16[4,8,16,1536]{3,2,1,0:T(8,128)(2,1)}), bf16[4,8,16,1536]{3,2,1,0:T(8,128)(2,1)S(1)}, u32[]{:S(2)}, u32[]{:S(2)}) async-start(bf16[4,8,16,1536]{3,2,1,0:T(8,128)(2,1)} %bitcast.44), calls=%async_computation.2 | async-start | bytes 3145728 | tf_op jit(solution)/shard_map/all_to_all | solution.py:26
  106.2 6.1 %collective-permute-start.24 = (bf16[4,16,1536]{2,1,0:T(8,128)(2,1)S(1)}, bf16[4,16,1536]{2,1,0:T(8,128)(2,1)S(1)}, u32[]{:S(2)}, u32[]{:S(2)}) collective-permute-start(bf16[4,16,1536]{2,1,0:T(8,128)(2,1)S(1)} %fusion.10), channel_id=1, source_target_pairs={{4,0},{8,4},{12,8},{16,12},{20,16},{24,20},{28,24},{0,28},{5,1},{9... | collective-permute-start | bytes 589832 | tf_op jit(solution)/shard_map/ppermute | solution.py:35
  109.5 7.0 %collective-permute-start.28 = (bf16[4,16,1536]{2,1,0:T(8,128)(2,1)S(1)}, bf16[4,16,1536]{2,1,0:T(8,128)(2,1)S(1)}, u32[]{:S(2)}, u32[]{:S(2)}) collective-permute-start(bf16[4,16,1536]{2,1,0:T(8,128)(2,1)S(1)} %fusion.8), channel_id=1, source_target_pairs={{28,0},{0,4},{4,8},{8,12},{12,16},{16,20},{20,24},{24,28},{29,1},{... | collective-permute-start | bytes 589832 | tf_op jit(solution)/shard_map/ppermute | solution.py:35
  112.4 6.5 %collective-permute-start.25 = (bf16[4,16,1536]{2,1,0:T(8,128)(2,1)S(1)}, bf16[4,16,1536]{2,1,0:T(8,128)(2,1)S(1)}, u32[]{:S(2)}, u32[]{:S(2)}) collective-permute-start(bf16[4,16,1536]{2,1,0:T(8,128)(2,1)S(1)} %fusion.11), channel_id=1, source_target_pairs={{4,0},{8,4},{12,8},{16,12},{20,16},{24,20},{28,24},{0,28},{5,1},{9... | collective-permute-start | bytes 589832 | tf_op jit(solution)/shard_map/ppermute | solution.py:35
  116.5 7.1 %collective-permute-start.29 = (bf16[4,16,1536]{2,1,0:T(8,128)(2,1)S(1)}, bf16[4,16,1536]{2,1,0:T(8,128)(2,1)S(1)}, u32[]{:S(2)}, u32[]{:S(2)}) collective-permute-start(bf16[4,16,1536]{2,1,0:T(8,128)(2,1)S(1)} %fusion.9), channel_id=1, source_target_pairs={{28,0},{0,4},{4,8},{8,12},{12,16},{16,20},{20,24},{24,28},{29,1},{... | collective-permute-start | bytes 589832 | tf_op jit(solution)/shard_map/ppermute | solution.py:35
  118.9 7.0 %collective-permute-start.26 = (bf16[4,16,1536]{2,1,0:T(8,128)(2,1)S(1)}, bf16[4,16,1536]{2,1,0:T(8,128)(2,1)S(1)}, u32[]{:S(2)}, u32[]{:S(2)}) collective-permute-start(bf16[4,16,1536]{2,1,0:T(8,128)(2,1)S(1)} %fusion.12), channel_id=1, source_target_pairs={{4,0},{8,4},{12,8},{16,12},{20,16},{24,20},{28,24},{0,28},{5,1},{9... | collective-permute-start | bytes 589832 | tf_op jit(solution)/shard_map/ppermute | solution.py:35
  127.0 18.3 %all-to-all-start.3 = ((bf16[8,16,1536]{2,1,0:T(8,128)(2,1)}), bf16[8,16,1536]{2,1,0:T(8,128)(2,1)S(1)}, u32[]{:S(2)}, u32[]{:S(2)}) async-start(bf16[8,16,1536]{2,1,0:T(8,128)(2,1)} %reduce_sum.47), calls=%async_computation.3 | async-start | bytes 786432 | tf_op jit(solution)/shard_map/all_to_all | solution.py:26
  133.4 6.5 %collective-permute-start.30 = (bf16[16,1536]{1,0:T(8,128)(2,1)S(1)}, bf16[16,1536]{1,0:T(8,128)(2,1)S(1)}, u32[]{:S(2)}, u32[]{:S(2)}) collective-permute-start(bf16[16,1536]{1,0:T(8,128)(2,1)S(1)} %get-tuple-element.853), channel_id=1, source_target_pairs={{3,0},{0,1},{1,2},{2,3},{7,4},{4,5},{5,6},{6,7},{11,8},{8,9},{9,10... | collective-permute-start | bytes 147464 | tf_op jit(solution)/shard_map/ppermute | solution.py:35
  135.0 5.6 %collective-permute-start.31 = (bf16[16,1536]{1,0:T(8,128)(2,1)S(1)}, bf16[16,1536]{1,0:T(8,128)(2,1)S(1)}, u32[]{:S(2)}, u32[]{:S(2)}) collective-permute-start(bf16[16,1536]{1,0:T(8,128)(2,1)S(1)} %get-tuple-element.855), channel_id=1, source_target_pairs={{2,0},{3,1},{0,2},{1,3},{6,4},{7,5},{4,6},{5,7},{10,8},{11,9},{8,1... | collective-permute-start | bytes 147464 | tf_op jit(solution)/shard_map/ppermute | solution.py:35
  135.9 4.7 %collective-permute-start.32 = (bf16[16,1536]{1,0:T(8,128)(2,1)S(1)}, bf16[16,1536]{1,0:T(8,128)(2,1)S(1)}, u32[]{:S(2)}, u32[]{:S(2)}) collective-permute-start(bf16[16,1536]{1,0:T(8,128)(2,1)S(1)} %get-tuple-element.854), channel_id=1, source_target_pairs={{1,0},{2,1},{3,2},{0,3},{5,4},{6,5},{7,6},{4,7},{9,8},{10,9},{11,1... | collective-permute-start | bytes 147464 | tf_op jit(solution)/shard_map/ppermute | solution.py:35
